TPU v7x, 128 devices: a whole 4x4x4 slice. The times are simulated.
128 devices in a mesh: sp: 2 (over core), ep: 64 (over x, y, z).
Axes of the slice: x: 4, y: 4, z: 4, core: 2. Of those that a mesh axis runs over, the one named last changes fastest.
Arguments:
- tokens: bfloat16 [64, 256, 768], P('ep', 'sp'), may hold values from -6 to 6
- cotangent: bfloat16 [64, 256, 768], P('ep', 'sp'), may hold values from -6 to 6
- w_query: bfloat16 [768, 768], P(('sp', 'ep')), may hold values from -0.21875 to 0.21875
- w_key: bfloat16 [768, 768], P(('sp', 'ep')), may hold values from -0.21875 to 0.21875
- w_value: bfloat16 [768, 768], P(('sp', 'ep')), may hold values from -0.21875 to 0.21875
- w_output: bfloat16 [768, 768], P(('sp', 'ep')), may hold values from -1.25 to 1.25
- gain_attn: bfloat16 [768], P(('sp', 'ep')), may hold values from 0.25 to 1.75
- gain_ffn: bfloat16 [768], P(('sp', 'ep')), may hold values from 0.25 to 1.75
- router: bfloat16 [768, 64], P(('sp', 'ep')), may hold values from -0.15625 to 0.15625
- bias_table: bfloat16 [384], P(('sp', 'ep')), may hold values from -4 to 4
- w_in: bfloat16 [64, 768, 3072], P('ep', None, 'sp'), may hold values from -0.21875 to 0.21875
- w_out: bfloat16 [64, 3072, 768], P('ep', 'sp'), may hold values from -0.109375 to 0.109375
- routes: int32 [64, 256, 2], P('ep', 'sp'), may hold values from 0 to 63, all different within a row; in each aligned block of 128 rows (0 to 127, 128 to 255, ..., all dimensions but the last counted through in order) at most 6 rows name the same one
- buckets: int32 [256], replicated, may hold values from 0 to 31
Outputs:
- mixed: bfloat16 [64, 256, 768], P('ep', 'sp')
- d_tokens: float32 [64, 256, 768], P('ep', 'sp')
- grad_w_query: float32 [768, 768], P(('sp', 'ep'))
- grad_w_key: float32 [768, 768], P(('sp', 'ep'))
- grad_w_value: float32 [768, 768], P(('sp', 'ep'))
- grad_w_output: float32 [768, 768], P(('sp', 'ep'))
- grad_gain_attn: float32 [768], P(('sp', 'ep'))
- grad_gain_ffn: float32 [768], P(('sp', 'ep'))
- grad_router: float32 [768, 64], P(('sp', 'ep'))
- grad_bias_table: float32 [384], P(('sp', 'ep'))
- grad_w_in: float32 [64, 768, 3072], P('ep', None, 'sp')
- grad_w_out: float32 [64, 3072, 768], P('ep', 'sp')
Inputs may be any that keep to these rules, and one draw needn't show every extreme that they name: `routes`: each row names two different experts; in the rows of one device (aligned blocks of 128 tokens in the order of sequences and positions) no expert is named by more than 6 rows.
All inputs are finite; a program needn't handle non-finite values.
Results may differ from a plain program's by a relative error of at most 0.024.
Values may be sent and summed in bfloat16 or wider, within the bound.
A program may use at most 192 MiB of HBM per device.

v0:
```python
import jax
import jax.numpy as jnp
from jax import lax
from jax.sharding import PartitionSpec as P

H = 12
HD = 64
NB = 32


epsilon = 1e-06
highest = lax.Precision.HIGHEST


def rms_norm(values, gain):
    return values * lax.rsqrt(jnp.mean(values * values, axis=-1, keepdims=True) + epsilon) * gain


def diagonal_sums(grid):
    heads_here, length, _ = grid.shape
    flipped = jnp.pad(grid[:, :, ::-1], ((0, 0), (0, 0), (0, length)))
    skewed = flipped.reshape(heads_here, 2 * length * length)[:, : length * (2 * length - 1)]
    skewed = skewed.reshape(heads_here, length, 2 * length - 1)
    return jnp.sum(skewed, axis=1)[:, length - 1 :]


def head_scores(query_heads, key_heads, bias, causal, scaling):
    scores = (
        jnp.einsum("qhd,khd->hqk", query_heads, key_heads, preferred_element_type=jnp.float32)
        * scaling
        + bias
    )
    return jnp.where(causal[None], scores, -jnp.inf)


def shards(
    tokens,
    cotangent,
    w_query,
    w_key,
    w_value,
    w_output,
    gain_attn,
    gain_ffn,
    router,
    bias_table,
    w_in,
    w_out,
    routes,
    buckets,
):
    sp_count = lax.axis_size("sp")
    ep_count = lax.axis_size("ep")
    tok_count = tokens.shape[1]
    width = tokens.shape[2]
    sources = sp_count * ep_count
    experts_all = router.shape[1]
    exp_local = w_in.shape[0]
    capacity = max(2, 3 * tok_count // experts_all)
    group_rows = exp_local * capacity
    heads_here = H // sp_count
    scaling = HD ** (-0.5)
    gathered = (
        lax.all_gather(w_query, ("sp", "ep"), axis=0, tiled=True),
        lax.all_gather(w_key, ("sp", "ep"), axis=0, tiled=True),
        lax.all_gather(w_value, ("sp", "ep"), axis=0, tiled=True),
        lax.all_gather(w_output, ("sp", "ep"), axis=0, tiled=True),
        lax.all_gather(router, ("sp", "ep"), axis=0, tiled=True),
        lax.all_gather(gain_attn, ("sp", "ep"), axis=0, tiled=True),
        lax.all_gather(gain_ffn, ("sp", "ep"), axis=0, tiled=True),
        lax.all_gather(bias_table, ("sp", "ep"), axis=0, tiled=True),
    )
    (
        query_full,
        key_full,
        value_full,
        output_full,
        router_full,
        gain_first,
        gain_second,
        table_full,
    ) = gathered
    gain_first = gain_first.astype(jnp.float32)
    gain_second = gain_second.astype(jnp.float32)
    inputs = tokens[0].astype(jnp.float32)
    normed_attn = rms_norm(inputs, gain_first).astype(jnp.bfloat16)
    query_tok = jnp.dot(normed_attn, query_full, preferred_element_type=jnp.float32).astype(
        jnp.bfloat16
    )
    key_tok = jnp.dot(normed_attn, key_full, preferred_element_type=jnp.float32).astype(
        jnp.bfloat16
    )
    value_tok = jnp.dot(normed_attn, value_full, preferred_element_type=jnp.float32).astype(
        jnp.bfloat16
    )
    query_seq, key_seq, value_seq = (
        lax.all_to_all(query_tok, "sp", split_axis=1, concat_axis=0, tiled=True),
        lax.all_to_all(key_tok, "sp", split_axis=1, concat_axis=0, tiled=True),
        lax.all_to_all(value_tok, "sp", split_axis=1, concat_axis=0, tiled=True),
    )
    seq_len = query_seq.shape[0]
    local_width = query_seq.shape[1]
    query_heads = query_seq.reshape(seq_len, heads_here, HD)
    key_heads = key_seq.reshape(seq_len, heads_here, HD)
    value_heads = value_seq.reshape(seq_len, heads_here, HD)
    head_first = lax.axis_index("sp") * heads_here
    table_local = lax.dynamic_slice_in_dim(
        table_full.astype(jnp.float32).reshape(NB, H), head_first, heads_here, 1
    )
    bucket_hot = (buckets[:, None] == jnp.arange(NB, dtype=jnp.int32)[None, :]).astype(jnp.float32)
    distance_bias = jnp.dot(bucket_hot, table_local, precision=highest).T
    places = jnp.arange(seq_len, dtype=jnp.int32)
    relative = jnp.maximum(places[:, None] - places[None, :], 0)
    causal = places[None, :] <= places[:, None]
    bias = jnp.take(distance_bias, relative, axis=1)
    scores = head_scores(query_heads, key_heads, bias, causal, scaling)
    peak = jnp.max(scores, axis=-1, keepdims=True)
    expanded = jnp.exp(scores - peak)
    totals = jnp.sum(expanded, axis=-1, keepdims=True)
    probs = expanded / totals
    log_total = peak + jnp.log(totals)
    probs_low = probs.astype(jnp.bfloat16)
    attended_seq = jnp.einsum(
        "hqk,khd->qhd", probs_low, value_heads, preferred_element_type=jnp.float32
    )
    attended_seq = attended_seq.astype(jnp.bfloat16).reshape(seq_len, local_width)
    attended = lax.all_to_all(attended_seq, "sp", split_axis=0, concat_axis=1, tiled=True)
    resid = inputs + jnp.dot(attended, output_full, preferred_element_type=jnp.float32)
    normed_ffn = rms_norm(resid, gain_second).astype(jnp.bfloat16)
    logits = jnp.dot(normed_ffn, router_full, preferred_element_type=jnp.float32)
    my_routes = routes[0]
    picked = (
        my_routes[:, :, None] == jnp.arange(experts_all, dtype=jnp.int32)[None, None, :]
    ).astype(jnp.float32)
    chosen = jnp.einsum("te,tke->tk", logits, picked, precision=highest)
    gates = jax.nn.softmax(chosen, axis=-1)
    flat_routes = my_routes.reshape(-1)
    route_hot = (flat_routes[:, None] == jnp.arange(experts_all, dtype=jnp.int32)[None, :]).astype(
        jnp.int32
    )
    ranking = jnp.sum((jnp.cumsum(route_hot, axis=0) - 1) * route_hot, axis=1)
    position = flat_routes * capacity + ranking

    def to_owners(rows_bf):
        filled = jnp.zeros((experts_all * capacity, width), jnp.bfloat16).at[position].set(rows_bf)
        doubled = jnp.broadcast_to(
            filled.reshape(1, ep_count, group_rows, width), (sp_count, ep_count, group_rows, width)
        )
        return doubled.reshape(sources, group_rows, width)

    def by_expert(arrived_rows):
        return (
            arrived_rows.reshape(sources, exp_local, capacity, width)
            .transpose(1, 0, 2, 3)
            .reshape(exp_local, sources * capacity, width)
        )

    def by_source(expert_major):
        return (
            expert_major.reshape(exp_local, sources, capacity, width)
            .transpose(1, 0, 2, 3)
            .reshape(sources, group_rows, width)
        )

    arrived = lax.all_to_all(
        to_owners(jnp.repeat(normed_ffn, 2, axis=0)),
        ("sp", "ep"),
        split_axis=0,
        concat_axis=0,
        tiled=True,
    )
    expert_rows = by_expert(arrived)
    pre_act = jnp.einsum("erd,edf->erf", expert_rows, w_in, preferred_element_type=jnp.float32)
    act_low = jax.nn.gelu(pre_act).astype(jnp.bfloat16)
    partial_out = by_source(
        jnp.einsum("erf,efd->erd", act_low, w_out, preferred_element_type=jnp.float32)
    )
    returned = lax.all_to_all(
        partial_out.astype(jnp.bfloat16), ("sp", "ep"), split_axis=0, concat_axis=0, tiled=True
    ).astype(partial_out.dtype)
    combined = jnp.sum(returned.reshape(sp_count, ep_count * group_rows, width), axis=0)
    expert_out = combined[position].reshape(tok_count, 2, width)
    mixed = resid + jnp.sum(gates[:, :, None] * expert_out, axis=1)
    query_back, key_back, value_back, output_back, router_back = (
        lax.all_gather(w_query, ("sp", "ep"), axis=0, tiled=True),
        lax.all_gather(w_key, ("sp", "ep"), axis=0, tiled=True),
        lax.all_gather(w_value, ("sp", "ep"), axis=0, tiled=True),
        lax.all_gather(w_output, ("sp", "ep"), axis=0, tiled=True),
        lax.all_gather(router, ("sp", "ep"), axis=0, tiled=True),
    )
    upstream = cotangent[0].astype(jnp.float32)
    d_gates = jnp.sum(expert_out * upstream[:, None, :], axis=-1)
    d_expert_out = (
        (gates[:, :, None] * upstream[:, None, :])
        .astype(jnp.bfloat16)
        .reshape(2 * tok_count, width)
    )
    d_arrived = lax.all_to_all(
        to_owners(d_expert_out), ("sp", "ep"), split_axis=0, concat_axis=0, tiled=True
    )
    d_rows = by_expert(d_arrived)
    d_act = jnp.einsum("erd,efd->erf", d_rows, w_out, preferred_element_type=jnp.float32)
    _, gelu_pull = jax.vjp(jax.nn.gelu, pre_act)
    d_pre = gelu_pull(d_act)[0].astype(jnp.bfloat16)
    grad_w_out = jnp.einsum("erf,erd->efd", act_low, d_rows, preferred_element_type=jnp.float32)
    grad_w_in = jnp.einsum("erd,erf->edf", expert_rows, d_pre, preferred_element_type=jnp.float32)
    d_partial = by_source(
        jnp.einsum("erf,edf->erd", d_pre, w_in, preferred_element_type=jnp.float32)
    )
    d_returned = lax.all_to_all(d_partial, ("sp", "ep"), split_axis=0, concat_axis=0, tiled=True)
    d_combined = jnp.sum(d_returned.reshape(sp_count, ep_count * group_rows, width), axis=0)
    d_normed_ffn = jnp.sum(d_combined[position].reshape(tok_count, 2, width), axis=1)
    d_chosen = gates * (d_gates - jnp.sum(gates * d_gates, axis=-1, keepdims=True))
    d_logits = jnp.einsum("tk,tke->te", d_chosen, picked, precision=highest).astype(jnp.bfloat16)
    d_normed_ffn = d_normed_ffn + jnp.dot(
        d_logits, router_back.T, preferred_element_type=jnp.float32
    )
    grad_router = jnp.dot(normed_ffn.T, d_logits, preferred_element_type=jnp.float32)
    _, norm_pull = jax.vjp(rms_norm, resid, gain_second)
    d_resid_norm, grad_gain_ffn = norm_pull(d_normed_ffn)
    d_resid = upstream + d_resid_norm
    d_branch = d_resid.astype(jnp.bfloat16)
    grad_w_output = jnp.dot(attended.T, d_branch, preferred_element_type=jnp.float32)
    d_attended = jnp.dot(d_branch, output_back.T, preferred_element_type=jnp.float32).astype(
        jnp.bfloat16
    )
    d_attended_seq = lax.all_to_all(
        d_attended, "sp", split_axis=1, concat_axis=0, tiled=True
    ).reshape(seq_len, heads_here, HD)
    scores_again = head_scores(query_heads, key_heads, bias, causal, scaling)
    probs_again = jnp.exp(scores_again - log_total)
    probs_again_low = probs_again.astype(jnp.bfloat16)
    d_value = jnp.einsum(
        "hqk,qhd->khd", probs_again_low, d_attended_seq, preferred_element_type=jnp.float32
    )
    d_probs = jnp.einsum(
        "qhd,khd->hqk", d_attended_seq, value_heads, preferred_element_type=jnp.float32
    )
    row_dot = jnp.sum(probs_again * d_probs, axis=-1, keepdims=True)
    d_scores = (probs_again * (d_probs - row_dot)).astype(jnp.bfloat16)
    d_query = (
        jnp.einsum("hqk,khd->qhd", d_scores, key_heads, preferred_element_type=jnp.float32)
        * scaling
    )
    d_key = (
        jnp.einsum("hqk,qhd->khd", d_scores, query_heads, preferred_element_type=jnp.float32)
        * scaling
    )
    d_distance = diagonal_sums(d_scores.astype(jnp.float32))
    table_grad_local = jnp.dot(bucket_hot.T, d_distance.T, precision=highest)
    table_grad = lax.dynamic_update_slice(
        jnp.zeros((NB, H), jnp.float32), table_grad_local, (jnp.int32(0), head_first)
    ).reshape(-1)
    d_query_tok, d_key_tok, d_value_tok = (
        lax.all_to_all(
            d_query.astype(jnp.bfloat16).reshape(seq_len, local_width),
            "sp",
            split_axis=0,
            concat_axis=1,
            tiled=True,
        ),
        lax.all_to_all(
            d_key.astype(jnp.bfloat16).reshape(seq_len, local_width),
            "sp",
            split_axis=0,
            concat_axis=1,
            tiled=True,
        ),
        lax.all_to_all(
            d_value.astype(jnp.bfloat16).reshape(seq_len, local_width),
            "sp",
            split_axis=0,
            concat_axis=1,
            tiled=True,
        ),
    )
    d_normed_attn = jnp.dot(d_query_tok, query_back.T, preferred_element_type=jnp.float32)
    d_normed_attn = d_normed_attn + jnp.dot(
        d_key_tok, key_back.T, preferred_element_type=jnp.float32
    )
    d_normed_attn = d_normed_attn + jnp.dot(
        d_value_tok, value_back.T, preferred_element_type=jnp.float32
    )
    grad_w_query = jnp.dot(normed_attn.T, d_query_tok, preferred_element_type=jnp.float32)
    grad_w_key = jnp.dot(normed_attn.T, d_key_tok, preferred_element_type=jnp.float32)
    grad_w_value = jnp.dot(normed_attn.T, d_value_tok, preferred_element_type=jnp.float32)
    _, first_pull = jax.vjp(rms_norm, inputs, gain_first)
    d_inputs_norm, grad_gain_attn = first_pull(d_normed_attn)
    d_tokens = (d_resid + d_inputs_norm).reshape(1, tok_count, width)
    summed = (
        lax.psum_scatter(grad_w_query, ("sp", "ep"), scatter_dimension=0, tiled=True),
        lax.psum_scatter(grad_w_key, ("sp", "ep"), scatter_dimension=0, tiled=True),
        lax.psum_scatter(grad_w_value, ("sp", "ep"), scatter_dimension=0, tiled=True),
        lax.psum_scatter(grad_w_output, ("sp", "ep"), scatter_dimension=0, tiled=True),
        lax.psum_scatter(grad_router, ("sp", "ep"), scatter_dimension=0, tiled=True),
        lax.psum_scatter(grad_gain_attn, ("sp", "ep"), scatter_dimension=0, tiled=True),
        lax.psum_scatter(grad_gain_ffn, ("sp", "ep"), scatter_dimension=0, tiled=True),
        lax.psum_scatter(table_grad, ("sp", "ep"), scatter_dimension=0, tiled=True),
    )
    return (
        mixed.astype(jnp.bfloat16).reshape(1, tok_count, width),
        d_tokens,
        summed[0],
        summed[1],
        summed[2],
        summed[3],
        summed[5],
        summed[6],
        summed[4],
        summed[7],
        grad_w_in,
        grad_w_out,
    )


def solution(mesh):
    placed = (
        P("ep", "sp", None),
        P("ep", "sp", None),
        P(("sp", "ep"), None),
        P(("sp", "ep"), None),
        P(("sp", "ep"), None),
        P(("sp", "ep"), None),
        P(("sp", "ep")),
        P(("sp", "ep")),
        P(("sp", "ep"), None),
        P(("sp", "ep")),
        P("ep", None, "sp"),
        P("ep", "sp", None),
        P("ep", "sp", None),
        P(),
    )
    return jax.shard_map(
        shards,
        mesh=mesh,
        in_specs=placed,
        out_specs=(
            P("ep", "sp", None),
            P("ep", "sp", None),
            P(("sp", "ep"), None),
            P(("sp", "ep"), None),
            P(("sp", "ep"), None),
            P(("sp", "ep"), None),
            P(("sp", "ep")),
            P(("sp", "ep")),
            P(("sp", "ep"), None),
            P(("sp", "ep")),
            P("ep", None, "sp"),
            P("ep", "sp", None),
        ),
        check_vma=False,
    )
```

profile of v0, /device:TPU:1, one launch (start us, length us, event | category | flops | bytes accessed | tf_op | source)
XLA Modules:
  0.0 1961.3 jit_solution(9700939576382141777)
XLA Ops:
  15.8 69.6 %all-reduce.18 = (bf16[768]{0:T(1024)(128)(2,1)S(1)}, bf16[32,12]{1,0:T(8,128)(2,1)S(1)}, bf16[768]{0:T(1024)(128)(2,1)S(1)}) all-reduce(bf16[768]{0:T(1024)(128)(2,1)S(1)} %dynamic-update-slice, bf16[32,12]{1,0:T(8,128)(2,1)S(1)} %reshape.394, bf16[768]{0:T(1024)(128)(2,1)S(1)} %dynamic-update-slice.2), channel_id=1, replica_groups=mesh['sp'=2,'ep'=64] {'sp','ep'}, use_global_device_ids=true, to_apply=%add.1 | all-reduce | flops 1920 | bytes 7680
  86.7 215.6 %gather_fusion = f32[65536,6]{1,0:T(8,128)} fusion(f32[6,256]{0,1:T(8,128)S(1)} %fusion.64, s32[65536]{0:T(1024)S(1)} %broadcast_clamp_fusion), kind=kCustom, calls=%fused_computation | custom fusion | bytes 3407872 | tf_op jit(solution)/shard_map/jit(_take)/gather | solution.py:115
  302.2 19.9 %copy.72 = f32[256,256,6]{0,1,2:T(8,128)} copy(f32[256,256,6]{2,1,0:T(8,128)} %bitcast.209) | data formatting | bytes 3145728 | tf_op jit(solution)/shard_map/jit(_take)/gather | solution.py:115
  384.8 339.3 %all-gather.4 = bf16[128,6,64]{2,1,0:T(8,128)(2,1)} all-gather(bf16[1,6,64]{2,1,0:T(8,128)(2,1)S(1)} %bitcast.252), channel_id=1, replica_groups=mesh['sp'=2,'ep'=64] {'sp','ep'}, dimensions={0}, use_global_device_ids=true | all-gather | bytes 99072 | tf_op jit(solution)/shard_map/all_gather | solution.py:68
  750.5 6.9 multiply_convert_fusion
  762.3 5.4 fusion.24
  770.0 10.5 all-to-all-start.5
  783.8 9.1 fusion.10
  805.6 10.5 all-to-all-start.7
  826.9 28.5 %all-to-all-done.7 = f32[128,6,768]{2,1,0:T(8,128)} async-done(((f32[128,6,768]{2,1,0:T(8,128)}), f32[128,6,768]{2,1,0:T(8,128)}, u32[]{:S(2)}, u32[]{:S(2)}) %all-to-all-start.7) | async-done | bytes 2359328 | tf_op jit(solution)/shard_map/all_to_all | solution.py:210
  897.3 395.0 %fusion.96 = (f32[8,768]{1,0:T(8,128)S(1)}, f32[8,768]{1,0:T(8,128)S(1)}, f32[8,768]{1,0:T(8,128)S(1)}, f32[8,768]{1,0:T(8,128)}) fusion(f32[768,768]{1,0:T(8,128)} %fusion.91, f32[768,768]{1,0:T(8,128)} %fusion.89, f32[768,768]{1,0:T(8,128)} %fusion.87, f32[768,768]{1,0:T(8,128)} %fusion.65), kind=kCustom, calls=%all-reduce-scatter.4 | all-reduce-scatter fusion | flops 3145729 | bytes 9535488
  1296.4 6.9 collective-permute-start.95
  1303.3 8.4 collective-permute-start.30
  1321.9 5.5 collective-permute-done.127
  1459.9 5.9 convolution_bitcast_fusion.1
  1495.4 6.2 convolution_bitcast_fusion
  1511.5 124.5 %all-reduce.22.cloned.1.call-done = f32[768,64]{1,0:T(8,128)} async-done(((f32[768,64]{1,0:T(8,128)}), f32[768,64]{1,0:T(8,128)}) %all-reduce.22.cloned.1.call-update) | async-done | bytes 196624
  1649.1 6.7 collective-permute-start.78
  1732.4 6.5 reshape.412
  1752.8 73.2 %all-reduce.17 = (f32[768]{0:T(1024)S(1)}, f32[768]{0:T(1024)S(1)}, f32[384]{0:T(512)S(1)}) all-reduce(f32[768]{0:T(1024)S(1)} %get-tuple-element.16, f32[768]{0:T(1024)S(1)} %copy-done.163, f32[384]{0:T(512)S(1)} %reshape.413), channel_id=6, replica_groups=mesh['sp'=2,'ep'=64] {'sp','ep'}, use_global_device_ids=true, to_apply=%region_25.26.clone | all-reduce | flops 1920 | bytes 15360
  1851.4 23.5 %concatenate.1 = f32[262,768]{1,0:T(8,128)S(1)} concatenate(f32[6,768]{1,0:T(8,128)S(1)} %copy-done.42, f32[8,768]{1,0:T(8,128)S(1)} %copy-done.96, f32[8,768]{1,0:T(8,128)S(1)} %copy-done.100, f32[8,768]{1,0:T(8,128)S(1)} %copy-done.104, f32[8,768]{1,0:T(8,128)S(1)} %copy-done.108, f32[8,768]{1,0:T(8,128)} %copy-done.111, f32[8,768]{1,0:T(8,128)} %copy-done.113, ...), dimensions={0} | concatenate | bytes 1609728
  1889.2 24.2 %concatenate.2 = f32[262,768]{1,0:T(8,128)S(1)} concatenate(f32[6,768]{1,0:T(8,128)S(1)} %copy-done.40, f32[8,768]{1,0:T(8,128)} %copy-done.118, f32[8,768]{1,0:T(8,128)} %copy-done.120, f32[8,768]{1,0:T(8,128)S(1)} %collective-permute-done.92, f32[8,768]{1,0:T(8,128)S(1)} %collective-permute-done.91, f32[8,768]{1,0:T(8,128)S(1)} %collective-permute-done.90, ...), dimensions={0} | concatenate | bytes 1609728
  1928.9 5.8 collective-permute-done.97
  1936.4 17.5 concatenate.3
  (783 shorter events, 517.5 us)
Async XLA Ops:
  7.2 316.1 %all-gather.10.cloned.1.call-start = ((), (), s32[]{:S(2)}) async-start(), calls=%async_computation.12 | async-start | bytes 1585152 | tf_op jit(solution)/shard_map/all_gather | solution.py:66
  7.9 325.0 %all-gather.12.cloned.1.call-start = ((), (), s32[]{:S(2)}) async-start(), calls=%async_computation.13 | async-start | bytes 1585152 | tf_op jit(solution)/shard_map/all_gather | solution.py:64
  8.7 333.5 %all-gather.14.cloned.1.call-start = ((), (), s32[]{:S(2)}) async-start(), calls=%async_computation.14 | async-start | bytes 1585152 | tf_op jit(solution)/shard_map/all_gather | solution.py:65
  9.4 350.3 %all-gather.16.cloned.1.call-start = ((), (), s32[]{:S(2)}) async-start(), calls=%async_computation.15 | async-start | bytes 1585152 | tf_op jit(solution)/shard_map/all_gather | solution.py:67
  375.1 365.0 %all-to-all-start.4 = ((bf16[128,6,768]{2,1,0:T(8,128)(2,1)}), bf16[128,6,768]{2,1,0:T(8,128)(2,1)}, u32[]{:S(2)}, u32[]{:S(2)}) async-start(bf16[128,6,768]{2,1,0:T(8,128)(2,1)} %bitcast.211), calls=%async_computation.4 | async-start | bytes 3145728 | tf_op jit(solution)/shard_map/all_to_all | solution.py:165
  805.6 49.8 %all-to-all-start.7 = ((f32[128,6,768]{2,1,0:T(8,128)}), f32[128,6,768]{2,1,0:T(8,128)}, u32[]{:S(2)}, u32[]{:S(2)}) async-start(f32[128,6,768]{2,1,0:T(8,128)} %copy.83), calls=%async_computation.7 | async-start | bytes 6291456 | tf_op jit(solution)/shard_map/all_to_all | solution.py:210
  893.2 742.7 %all-reduce.22.cloned.1.call-start = ((), (), s32[]{:S(2)}) async-start(), calls=%async_computation.16 | async-start | bytes 786432
  1501.6 135.6 %collective-permute-start.87 = (f32[8,768]{1,0:T(8,128)S(1)}, f32[8,768]{1,0:T(8,128)S(1)}, u32[]{:S(2)}, u32[]{:S(2)}) collective-permute-start(f32[8,768]{1,0:T(8,128)S(1)} %get-tuple-element.30), channel_id=1, source_target_pairs={{0,24},{1,25},{2,26},{3,27},{4,28},{5,29},{6,30},{7,31},{8,32},{9,... | collective-permute-start | bytes 73736
  1503.7 138.2 %collective-permute-start.86 = (f32[8,768]{1,0:T(8,128)S(1)}, f32[8,768]{1,0:T(8,128)S(1)}, u32[]{:S(2)}, u32[]{:S(2)}) collective-permute-start(f32[8,768]{1,0:T(8,128)S(1)} %get-tuple-element.30), channel_id=1, source_target_pairs={{0,23},{1,24},{2,25},{3,26},{4,27},{5,28},{6,29},{7,30},{8,31},{9,... | collective-permute-start | bytes 73736
  1505.6 138.7 %collective-permute-start.85 = (f32[8,768]{1,0:T(8,128)S(1)}, f32[8,768]{1,0:T(8,128)S(1)}, u32[]{:S(2)}, u32[]{:S(2)}) collective-permute-start(f32[8,768]{1,0:T(8,128)S(1)} %get-tuple-element.30), channel_id=1, source_target_pairs={{0,22},{1,23},{2,24},{3,25},{4,26},{5,27},{6,28},{7,29},{8,30},{9,... | collective-permute-start | bytes 73736
  1507.6 139.6 %collective-permute-start.84 = (f32[8,768]{1,0:T(8,128)S(1)}, f32[8,768]{1,0:T(8,128)S(1)}, u32[]{:S(2)}, u32[]{:S(2)}) collective-permute-start(f32[8,768]{1,0:T(8,128)S(1)} %get-tuple-element.30), channel_id=1, source_target_pairs={{0,21},{1,22},{2,23},{3,24},{4,25},{5,26},{6,27},{7,28},{8,29},{9,... | collective-permute-start | bytes 73736
  1509.5 139.6 %collective-permute-start.83 = (f32[8,768]{1,0:T(8,128)S(1)}, f32[8,768]{1,0:T(8,128)S(1)}, u32[]{:S(2)}, u32[]{:S(2)}) collective-permute-start(f32[8,768]{1,0:T(8,128)S(1)} %get-tuple-element.30), channel_id=1, source_target_pairs={{0,20},{1,21},{2,22},{3,23},{4,24},{5,25},{6,26},{7,27},{8,28},{9,... | collective-permute-start | bytes 73736
  1741.6 91.3 %collective-permute-start.115 = (f32[8,768]{1,0:T(8,128)}, f32[8,768]{1,0:T(8,128)}, u32[]{:S(2)}, u32[]{:S(2)}) collective-permute-start(f32[8,768]{1,0:T(8,128)} %get-tuple-element.31), channel_id=1, source_target_pairs={{0,20},{1,21},{2,22},{3,23},{4,24},{5,25},{6,26},{7,27},{8,28},{9,... | collective-permute-start | bytes 73736
  1743.5 93.8 %collective-permute-start.114 = (f32[8,768]{1,0:T(8,128)}, f32[8,768]{1,0:T(8,128)}, u32[]{:S(2)}, u32[]{:S(2)}) collective-permute-start(f32[8,768]{1,0:T(8,128)} %get-tuple-element.31), channel_id=1, source_target_pairs={{0,19},{1,20},{2,21},{3,22},{4,23},{5,24},{6,25},{7,26},{8,27},{9,... | collective-permute-start | bytes 73736
  1745.5 94.2 %collective-permute-start.113 = (f32[8,768]{1,0:T(8,128)}, f32[8,768]{1,0:T(8,128)}, u32[]{:S(2)}, u32[]{:S(2)}) collective-permute-start(f32[8,768]{1,0:T(8,128)} %get-tuple-element.31), channel_id=1, source_target_pairs={{0,18},{1,19},{2,20},{3,21},{4,22},{5,23},{6,24},{7,25},{8,26},{9,... | collective-permute-start | bytes 73736
  1747.4 94.2 %collective-permute-start.112 = (f32[8,768]{1,0:T(8,128)}, f32[8,768]{1,0:T(8,128)}, u32[]{:S(2)}, u32[]{:S(2)}) collective-permute-start(f32[8,768]{1,0:T(8,128)} %get-tuple-element.31), channel_id=1, source_target_pairs={{0,17},{1,18},{2,19},{3,20},{4,21},{5,22},{6,23},{7,24},{8,25},{9,... | collective-permute-start | bytes 73736
  1749.4 96.6 %collective-permute-start.111 = (f32[8,768]{1,0:T(8,128)}, f32[8,768]{1,0:T(8,128)}, u32[]{:S(2)}, u32[]{:S(2)}) collective-permute-start(f32[8,768]{1,0:T(8,128)} %get-tuple-element.31), channel_id=1, source_target_pairs={{0,16},{1,17},{2,18},{3,19},{4,20},{5,21},{6,22},{7,23},{8,24},{9,... | collective-permute-start | bytes 73736
  1832.9 42.0 %collective-permute-start.110 = (f32[8,768]{1,0:T(8,128)}, f32[8,768]{1,0:T(8,128)}, u32[]{:S(2)}, u32[]{:S(2)}) collective-permute-start(f32[8,768]{1,0:T(8,128)} %get-tuple-element.31), channel_id=1, source_target_pairs={{0,15},{1,16},{2,17},{3,18},{4,19},{5,20},{6,21},{7,22},{8,23},{9,... | collective-permute-start | bytes 73736
  1837.3 40.9 %collective-permute-start.109 = (f32[8,768]{1,0:T(8,128)}, f32[8,768]{1,0:T(8,128)}, u32[]{:S(2)}, u32[]{:S(2)}) collective-permute-start(f32[8,768]{1,0:T(8,128)} %get-tuple-element.31), channel_id=1, source_target_pairs={{0,14},{1,15},{2,16},{3,17},{4,18},{5,19},{6,20},{7,21},{8,22},{9,... | collective-permute-start | bytes 73736
  1839.7 40.5 %collective-permute-start.108 = (f32[8,768]{1,0:T(8,128)}, f32[8,768]{1,0:T(8,128)}, u32[]{:S(2)}, u32[]{:S(2)}) collective-permute-start(f32[8,768]{1,0:T(8,128)} %get-tuple-element.31), channel_id=1, source_target_pairs={{0,13},{1,14},{2,15},{3,16},{4,17},{5,18},{6,19},{7,20},{8,21},{9,... | collective-permute-start | bytes 73736
  1841.6 41.1 %collective-permute-start.107 = (f32[8,768]{1,0:T(8,128)}, f32[8,768]{1,0:T(8,128)}, u32[]{:S(2)}, u32[]{:S(2)}) collective-permute-start(f32[8,768]{1,0:T(8,128)} %get-tuple-element.31), channel_id=1, source_target_pairs={{0,12},{1,13},{2,14},{3,15},{4,16},{5,17},{6,18},{7,19},{8,20},{9,... | collective-permute-start | bytes 73736
  1846.0 39.8 %collective-permute-start.106 = (f32[8,768]{1,0:T(8,128)}, f32[8,768]{1,0:T(8,128)}, u32[]{:S(2)}, u32[]{:S(2)}) collective-permute-start(f32[8,768]{1,0:T(8,128)} %get-tuple-element.31), channel_id=1, source_target_pairs={{0,11},{1,12},{2,13},{3,14},{4,15},{5,16},{6,17},{7,18},{8,19},{9,... | collective-permute-start | bytes 73736
  1882.8 40.9 %collective-permute-start.102 = (f32[8,768]{1,0:T(8,128)}, f32[8,768]{1,0:T(8,128)S(1)}, u32[]{:S(2)}, u32[]{:S(2)}) collective-permute-start(f32[8,768]{1,0:T(8,128)} %get-tuple-element.31), channel_id=1, source_target_pairs={{0,7},{1,8},{2,9},{3,10},{4,11},{5,12},{6,13},{7,14},{8,15},{9,16}... | collective-permute-start | bytes 73736
  1885.9 39.7 %collective-permute-start.101 = (f32[8,768]{1,0:T(8,128)}, f32[8,768]{1,0:T(8,128)S(1)}, u32[]{:S(2)}, u32[]{:S(2)}) collective-permute-start(f32[8,768]{1,0:T(8,128)} %get-tuple-element.31), channel_id=1, source_target_pairs={{0,6},{1,7},{2,8},{3,9},{4,10},{5,11},{6,12},{7,13},{8,14},{9,15},... | collective-permute-start | bytes 73736
  (295 other events, 13623.8 us)
Sparse Core Ops, SparseCore 0:
  10.8 67.8 all-gather.9
  81.5 61.5 all-gather.11
  145.9 61.5 all-gather.13
  210.2 61.5 all-gather.15
  1480.4 155.4 all-reduce.21
where the time goes:
time: 1990 us; the launch traced here: 1960 us
  blocking collectives  894 us (45%)
  local copies, waits for them, and re-layouts  405 us (20%)
  starting transfers between devices  356 us (18%)
  waiting for transfers between devices  193 us (10%)
  matrix products  70.9 us (4%)
  other arithmetic  23.7 us (1%)
    unnamed x3, blocking collectives  538 us
    all_gather x1, blocking collectives, shards(): lax.all_gather(router, ('sp', 'ep'), axis=0, tiled=True)  339 us
    unnamed x129, starting transfers between devices  310 us
    gather x2, local copies, waits for them, and re-layouts, shards(): bias = jnp.take(distance_bias, relative, axis=1)  235 us
    unnamed x134, waiting for transfers between devices  164 us
    unnamed x388, local copies, waits for them, and re-layouts  102 us
  transfers between devices with their start and end apart: 141, of which 22 were waited for; matrix products, arithmetic and copies ran while one was open for 23% of the time, Pallas kernels for 0%

commit v1 on v0

v1 whole, which is shorter than its diff:
```python
import functools

import jax
import jax.numpy as jnp
from jax import lax
from jax.experimental import pallas as pl
from jax.experimental.pallas import tpu as pltpu
from jax.sharding import PartitionSpec as P

D = 768
H = 12
HD = 64
HH = H // 2
HW = HH * HD
EXP = 64
EPS = 1e-06
SLOT = 8
QROW = 16
QW = 3 * HW
PW = QW + 128
ROUTER = QW
GAIN = QW + 64
F32 = jnp.float32
BF16 = jnp.bfloat16
VMEM_LIMIT = 56 * 1024 * 1024


def iota(shape, axis):
    return lax.broadcasted_iota(jnp.int32, shape, axis)


def nn(left, right):
    return lax.dot_general(left, right, (((1,), (0,)), ((), ())), preferred_element_type=F32)


def nt(left, right):
    return lax.dot_general(left, right, (((1,), (1,)), ((), ())), preferred_element_type=F32)


def tn(left, right):
    return lax.dot_general(left, right, (((0,), (0,)), ((), ())), preferred_element_type=F32)


def chunk_feature(rows):
    owner = jnp.right_shift(rows, 4)
    inner = jnp.bitwise_and(rows, 15)
    half = (inner >= 6).astype(jnp.int32)
    feature = half * (D // 2) + owner * 6 + inner - 6 * half
    return jnp.where(inner < 12, feature, -1)


def chunk_entry(rows):
    owner = jnp.right_shift(rows, 4)
    inner = jnp.bitwise_and(rows, 15)
    half = (inner >= 6).astype(jnp.int32)
    inside = inner - 6 * half
    entry = half * (32 * H // 2) + owner * 3 + inside
    return jnp.where((inner < 12) & (inside < 3), entry, -1)


def hot(condition):
    return jnp.where(condition, 1.0, 0.0).astype(BF16)


def to_chunks():
    rows = iota((D, EXP * QROW), 1)
    return hot(chunk_feature(rows) == iota((D, EXP * QROW), 0))


def from_chunks():
    rows = iota((EXP * QROW, D), 0)
    return hot(chunk_feature(rows) == iota((EXP * QROW, D), 1))


def rms_of(values):
    return lax.rsqrt(jnp.mean(values * values, axis=-1, keepdims=True) + EPS)


def head_bias(bias_ref, head, seq):
    row = jnp.broadcast_to(bias_ref[head : head + 1, :], (seq, seq))
    return pltpu.roll(row, 0, 1, stride=1, stride_axis=0)


def first_kernel(seq_ref, pack_ref, bucket_ref, attended_ref, qkv_ref, full_ref, gains_ref, normed_ref, bias_ref, lse_ref):
    seq = seq_ref.shape[0]
    sp = lax.axis_index("sp")
    spread = to_chunks()
    full_ref[...] = nn(spread, pack_ref[...]).astype(BF16)
    tail = pack_ref[:, QW:]
    gains = tn(tail, from_chunks())
    gains_ref[...] = gains
    rows = iota((EXP * QROW, 128), 0)
    entry = chunk_entry(rows)
    bucket_of = jnp.right_shift(entry * 5462, 16)
    head_of = entry - bucket_of * H
    column = iota((EXP * QROW, 128), 1)
    table = jnp.where(
        (entry >= 0) & (head_of == sp * HH + column) & (column < HH),
        tail[:, 66:67].astype(F32),
        0.0,
    ).astype(BF16)
    entry_wide = chunk_entry(iota((EXP * QROW, seq), 0))
    bucket_wide = jnp.where(entry_wide >= 0, jnp.right_shift(entry_wide * 5462, 16), -1)
    bias_ref[...] = tn(table, hot(bucket_wide == bucket_ref[0:1, :]))[0:8, :]

    inputs = seq_ref[...].astype(F32)
    normed = (inputs * rms_of(inputs) * gains[64:65, :]).astype(BF16)
    normed_ref[...] = normed
    qkv_ref[...] = nn(normed, full_ref[:, :QW]).astype(BF16)
    causal = iota((seq, seq), 1) <= iota((seq, seq), 0)
    lse_ref[...] = jnp.zeros_like(lse_ref)
    for head in range(HH):
        at = head * HD
        query = qkv_ref[:, at : at + HD]
        key = qkv_ref[:, HW + at : HW + at + HD]
        value = qkv_ref[:, 2 * HW + at : 2 * HW + at + HD]
        scores = nt(query, key) * (HD**-0.5) + head_bias(bias_ref, head, seq)
        scores = jnp.where(causal, scores, -jnp.inf)
        peak = jnp.max(scores, axis=-1, keepdims=True)
        grown = jnp.exp(scores - peak)
        total = jnp.sum(grown, axis=-1, keepdims=True)
        probs = (grown / total).astype(BF16)
        attended_ref[:, at : at + HD] = nn(probs, value).astype(BF16)
        lse_ref[:, head : head + 1] = peak + jnp.log(total)


def route_hot(routes_ref, k, width):
    return (routes_ref[:, k : k + 1] == iota((routes_ref.shape[0], width), 1)).astype(F32)


def middle_kernel(parts_ref, tok_ref, cot_ref, gains_ref, full_ref, routes_ref, filled_ref, resid_ref, normed_ref, places_ref, gates_ref):
    count = tok_ref.shape[0]
    resid = tok_ref[...].astype(F32) + parts_ref[:count, :] + parts_ref[count:, :]
    resid_ref[...] = resid
    normed = (resid * rms_of(resid) * gains_ref[65:66, :]).astype(BF16)
    normed_ref[...] = normed
    logits = nn(normed, full_ref[:, ROUTER : ROUTER + EXP])
    named = [route_hot(routes_ref, k, EXP) for k in range(2)]
    chosen = [jnp.sum(logits * one, axis=-1, keepdims=True) for one in named]
    peak = jnp.maximum(chosen[0], chosen[1])
    grown = [jnp.exp(one - peak) for one in chosen]
    total = grown[0] + grown[1]
    gates = [one / total for one in grown]
    column = iota((count, 128), 1)
    gates_ref[...] = jnp.where(column == 0, gates[0], jnp.where(column == 1, gates[1], 0.0))
    before = hot(iota((count, count), 1) < iota((count, count), 0))
    earlier = nn(before, (named[0] + named[1]).astype(BF16))
    upstream = cot_ref[...].astype(F32)
    slots = iota((count, EXP * SLOT), 1)
    filled_d = jnp.zeros((EXP * SLOT, D), F32)
    either = jnp.zeros((count, EXP * SLOT), F32)
    for k in range(2):
        rank = jnp.sum(earlier * named[k], axis=-1, keepdims=True).astype(jnp.int32)
        place = (slots == routes_ref[:, k : k + 1] * SLOT + rank).astype(F32)
        either = either + place
        places_ref[:, k * EXP * SLOT : (k + 1) * EXP * SLOT] = place.astype(BF16)
        filled_d = filled_d + tn(place.astype(BF16), (gates[k] * upstream).astype(BF16))
    filled_ref[:, :D] = tn(either.astype(BF16), normed).astype(BF16)
    filled_ref[:, D:] = filled_d.astype(BF16)


def expert_kernel(rows_ref, win_ref, wout_ref, result_ref, act_ref, dpre_ref, out_acc, back_acc):
    step = pl.program_id(0)

    @pl.when(step == 0)
    def _():
        out_acc[...] = jnp.zeros_like(out_acc)
        back_acc[...] = jnp.zeros_like(back_acc)

    first = win_ref[...]
    second = wout_ref[...]
    pre = nn(rows_ref[:, :D], first)
    square = pre * pre
    slope = 0.7978845608028654
    t = jnp.tanh(slope * (pre + 0.044715 * (square * pre)))
    half = 0.5 * (1.0 + t)
    act = (pre * half).astype(BF16)
    act_ref[...] = act
    out_acc[...] += nn(act, second)
    d_act = nt(rows_ref[:, D:], second)
    bend = half + 0.5 * pre * (1.0 - t * t) * (slope * (1.0 + 3 * 0.044715 * square))
    d_pre = (d_act * bend).astype(BF16)
    dpre_ref[...] = d_pre
    back_acc[...] += nt(d_pre, first)

    @pl.when(step == pl.num_programs(0) - 1)
    def _():
        result_ref[:, :D] = out_acc[...].astype(BF16)
        result_ref[:, D:] = back_acc[...].astype(BF16)


def expert_grad_kernel(rows_ref, act_ref, dpre_ref, gin_ref, gout_ref, turned):
    @pl.when(pl.program_id(0) == 0)
    def _():
        turned[...] = rows_ref[:, :D].T

    gin_ref[0] = nn(turned[...], dpre_ref[...])
    gout_ref[0] = tn(act_ref[...], rows_ref[:, D:])


def mix_kernel(ret_ref, places_ref, gates_ref, resid_ref, cot_ref, gains_ref, full_ref, normed_ref, routes_ref, mixed_ref, dresid_ref, dbranch_ref, grouter_ref, ggain_ref):
    count = resid_ref.shape[0]
    slots = EXP * SLOT
    resid = resid_ref[...]
    upstream = cot_ref[...].astype(F32)
    gates = [gates_ref[:, k : k + 1] for k in range(2)]
    outs = [nn(places_ref[:, k * slots : (k + 1) * slots], ret_ref[:, :D]) for k in range(2)]
    mixed_ref[0] = (resid + (gates[0] * outs[0] + gates[1] * outs[1])).astype(BF16)
    d_gates = [jnp.sum(one * upstream, axis=-1, keepdims=True) for one in outs]
    inner = gates[0] * d_gates[0] + gates[1] * d_gates[1]
    d_logits = jnp.zeros((count, EXP), F32)
    for k in range(2):
        d_logits = d_logits + route_hot(routes_ref, k, EXP) * (gates[k] * (d_gates[k] - inner))
    d_logits = d_logits.astype(BF16)
    either = places_ref[:, :slots] + places_ref[:, slots:]
    d_normed = nn(either, ret_ref[:, D:]) + nt(d_logits, full_ref[:, ROUTER : ROUTER + EXP])
    chunked = nn(normed_ref[...], to_chunks()).astype(BF16)
    grouter_ref[...] = tn(chunked, d_logits)
    rms = rms_of(resid)
    u = d_normed * gains_ref[65:66, :]
    d_resid = upstream + rms * u - resid * (rms * rms * rms) * jnp.mean(u * resid, axis=-1, keepdims=True)
    ggain_ref[...] = jnp.broadcast_to(jnp.sum(d_normed * resid * rms, axis=0, keepdims=True), ggain_ref.shape)
    dresid_ref[...] = d_resid
    dbranch_ref[...] = d_resid.astype(BF16)


def split_two(values):
    high = values.astype(BF16)
    return high, (values - high.astype(F32)).astype(BF16)


def last_kernel(branch_ref, wo_ref, qkv_ref, lse_ref, bias_ref, normed_ref, seq_ref, full_ref, bucket_ref, grouter_ref, gffn_ref, pack_ref, dnorm_ref, dqkv, ddist):
    seq = seq_ref.shape[0]
    sp = lax.axis_index("sp")
    d_attended = nt(branch_ref[...], wo_ref[...]).astype(BF16)
    causal = iota((seq, seq), 1) <= iota((seq, seq), 0)
    flip = hot(iota((seq, seq), 0) + iota((seq, seq), 1) == seq - 1)
    ddist[...] = jnp.zeros_like(ddist)
    for head in range(HH):
        at = head * HD
        query = qkv_ref[:, at : at + HD]
        key = qkv_ref[:, HW + at : HW + at + HD]
        value = qkv_ref[:, 2 * HW + at : 2 * HW + at + HD]
        d_out = d_attended[:, at : at + HD]
        scores = nt(query, key) * (HD**-0.5) + head_bias(bias_ref, head, seq)
        probs = jnp.where(causal, jnp.exp(scores - lse_ref[:, head : head + 1]), 0.0)
        d_value = tn(probs.astype(BF16), d_out)
        d_probs = nt(d_out, value)
        row_dot = jnp.sum(probs * d_probs, axis=-1, keepdims=True)
        d_scores = (probs * (d_probs - row_dot)).astype(BF16)
        dqkv[:, at : at + HD] = (nn(d_scores, key) * (HD**-0.5)).astype(BF16)
        dqkv[:, HW + at : HW + at + HD] = (tn(d_scores, query) * (HD**-0.5)).astype(BF16)
        dqkv[:, 2 * HW + at : 2 * HW + at + HD] = d_value.astype(BF16)
        skewed = pltpu.roll(nn(d_scores, flip), 0, 1, stride=1, stride_axis=0)
        ddist[head : head + 1, :] = jnp.sum(skewed, axis=0, keepdims=True)
    d_normed = nt(dqkv[...], full_ref[:, :QW])
    dnorm_ref[...] = d_normed
    chunked = nn(normed_ref[...], to_chunks()).astype(BF16)
    turned = chunked.T
    pack_ref[:, :QW] = nn(turned, dqkv[...]).astype(BF16)
    inputs = seq_ref[...].astype(F32)
    g_first = jnp.sum(d_normed * inputs * rms_of(inputs), axis=0, keepdims=True)
    order = from_chunks()
    first_high, first_low = split_two(jnp.broadcast_to(g_first, (16, D)))
    second_high, second_low = split_two(jnp.broadcast_to(gffn_ref[0:1, :], (16, D)))
    gains = [nt(order, one)[:, 0:1] for one in (first_high, first_low, second_high, second_low)]
    rows = iota((EXP * QROW, seq), 0)
    entry = chunk_entry(rows)
    bucket_wide = jnp.where(entry >= 0, jnp.right_shift(entry * 5462, 16), -1)
    pick = hot(bucket_wide == bucket_ref[1:2, :])
    high, low = split_two(ddist[...])
    by_head = nt(pick, high) + nt(pick, low)
    entry = chunk_entry(iota(by_head.shape, 0))
    head_of = entry - jnp.right_shift(entry * 5462, 16) * H
    mine = (entry >= 0) & (head_of == sp * HH + iota(by_head.shape, 1)) & (iota(by_head.shape, 1) < HH)
    table = jnp.sum(jnp.where(mine, by_head, 0.0), axis=-1, keepdims=True)
    table_high, table_low = split_two(table)
    column = iota((EXP * QROW, 64), 1)
    tail = jnp.zeros((EXP * QROW, 64), F32)
    for place, values in enumerate(gains + [table_high.astype(F32), table_low.astype(F32)]):
        tail = jnp.where(column == place, values, tail)
    pack_ref[:, QW:] = jnp.concatenate([grouter_ref[...], tail], axis=1).astype(BF16)


def end_kernel(parts_ref, dresid_ref, tok_ref, gains_ref, out_ref):
    count = tok_ref.shape[0]
    inputs = tok_ref[...].astype(F32)
    d_normed = parts_ref[:count, :] + parts_ref[count:, :]
    rms = rms_of(inputs)
    v = d_normed * gains_ref[64:65, :]
    out_ref[0] = dresid_ref[...] + rms * v - inputs * (rms * rms * rms) * jnp.mean(v * inputs, axis=-1, keepdims=True)


def whole(kernel, outs, scratch=(), flops=0, moved=0):
    return pl.pallas_call(
        kernel,
        out_shape=[jax.ShapeDtypeStruct(shape, kind) for shape, kind in outs],
        scratch_shapes=list(scratch),
        compiler_params=pltpu.CompilerParams(vmem_limit_bytes=VMEM_LIMIT),
        cost_estimate=pl.CostEstimate(flops=flops, bytes_accessed=moved, transcendentals=0),
    )


def swap(values, axis="sp"):
    return lax.all_to_all(values, axis, split_axis=0, concat_axis=0, tiled=True)


def shards(tokens, cotangent, w_query, w_key, w_value, w_output, gain_attn, gain_ffn, router, bias_table, w_in, w_out, routes, buckets):
    count = tokens.shape[1]
    seq = 2 * count
    owners = lax.axis_size("ep")
    tok = tokens[0]
    cot = cotangent[0]
    route = routes[0]
    qkv = jnp.concatenate([w_query, w_key, w_value], axis=1).reshape(6, 3, 2, HW)
    qkv = qkv.transpose(2, 0, 1, 3).reshape(2, 6, QW)
    tail = jnp.concatenate(
        [
            router,
            gain_attn[:, None],
            gain_ffn[:, None],
            jnp.pad(bias_table, (0, 3))[:, None],
            jnp.zeros((6, 61), BF16),
        ],
        axis=1,
    )
    chunk = jnp.concatenate([qkv, jnp.broadcast_to(tail[None], (2, 6, 128))], axis=2)
    chunk = jnp.pad(swap(chunk).reshape(12, PW), ((0, QROW - 12), (0, 0)))
    pack = swap(jnp.broadcast_to(chunk[None], (owners, QROW, PW)), "ep").reshape(owners * QROW, PW)
    out_chunk = jnp.pad(w_output, ((0, SLOT - 6), (0, 0)))
    out_pack = swap(jnp.broadcast_to(out_chunk[None], (owners, SLOT, D)), "ep").reshape(owners * SLOT, D)
    sequence = swap(jnp.broadcast_to(tok[None], (2, count, D))).reshape(seq, D)
    turned_buckets = jnp.stack([jnp.roll(buckets[::-1], 1), jnp.roll(buckets, -1)])

    attended, qkv_all, full, gains, normed_attn, bias, lse = whole(
        first_kernel,
        [
            ((seq, HW), BF16),
            ((seq, QW), BF16),
            ((D, PW), BF16),
            ((128, D), F32),
            ((seq, D), BF16),
            ((8, seq), F32),
            ((seq, 128), F32),
        ],
        flops=4 * 10**9,
        moved=8 * 10**6,
    )(sequence, pack, turned_buckets)

    place = jnp.arange(owners * SLOT, dtype=jnp.int32)
    owner_row = jnp.where(place % SLOT < 6, place // SLOT * 6 + place % SLOT, -1)
    gather_rows = (owner_row[None, :] == jnp.arange(HW, dtype=jnp.int32)[:, None]).astype(BF16)
    output_mine = nn(gather_rows, out_pack).astype(BF16)
    branch = nn(attended, output_mine)
    parts = swap(branch.reshape(2, count, D)).reshape(seq, D)

    filled, resid, normed_ffn, places, gates = whole(
        middle_kernel,
        [
            ((EXP * SLOT, 2 * D), BF16),
            ((count, D), F32),
            ((count, D), BF16),
            ((count, 2 * EXP * SLOT), BF16),
            ((count, 128), F32),
        ],
        flops=10**9,
        moved=4 * 10**6,
    )(parts, tok, cot, gains, full, route)

    arrived = swap(filled.reshape(owners, SLOT, 2 * D), "ep")
    rows = swap(jnp.broadcast_to(arrived.reshape(1, owners * SLOT, 2 * D), (2, owners * SLOT, 2 * D)))
    rows = rows.reshape(2 * owners * SLOT, 2 * D)
    load = rows.shape[0]
    hidden = w_in.shape[2]
    step = 256
    resident = pl.BlockSpec((load, 2 * D), lambda f: (0, 0))
    by_column = pl.BlockSpec((load, step), lambda f: (0, f))
    result, act, d_pre = pl.pallas_call(
        expert_kernel,
        grid=(hidden // step,),
        in_specs=[
            resident,
            pl.BlockSpec((D, step), lambda f: (0, f)),
            pl.BlockSpec((step, D), lambda f: (f, 0)),
        ],
        out_specs=[resident, by_column, by_column],
        out_shape=[
            jax.ShapeDtypeStruct((load, 2 * D), BF16),
            jax.ShapeDtypeStruct((load, hidden), BF16),
            jax.ShapeDtypeStruct((load, hidden), BF16),
        ],
        scratch_shapes=[pltpu.VMEM((load, D), F32), pltpu.VMEM((load, D), F32)],
        compiler_params=pltpu.CompilerParams(vmem_limit_bytes=VMEM_LIMIT),
        cost_estimate=pl.CostEstimate(flops=8 * load * D * hidden, bytes_accessed=20 * 10**6, transcendentals=load * hidden),
    )(rows, w_in[0], w_out[0])
    halves = swap(result.reshape(2, owners * SLOT, 2 * D))
    joined = (halves[0].astype(F32) + halves[1].astype(F32)).astype(BF16)
    returned = swap(joined.reshape(owners, SLOT, 2 * D), "ep").reshape(owners * SLOT, 2 * D)

    grad_w_in, grad_w_out = pl.pallas_call(
        expert_grad_kernel,
        grid=(hidden // step,),
        in_specs=[resident, by_column, by_column],
        out_specs=[
            pl.BlockSpec((1, D, step), lambda f: (0, 0, f)),
            pl.BlockSpec((1, step, D), lambda f: (0, f, 0)),
        ],
        out_shape=[
            jax.ShapeDtypeStruct((1, D, hidden), F32),
            jax.ShapeDtypeStruct((1, hidden, D), F32),
        ],
        scratch_shapes=[pltpu.VMEM((D, load), BF16)],
        compiler_params=pltpu.CompilerParams(vmem_limit_bytes=VMEM_LIMIT),
        cost_estimate=pl.CostEstimate(flops=4 * load * D * hidden, bytes_accessed=20 * 10**6, transcendentals=0),
    )(rows, act, d_pre)

    mixed, d_resid, d_branch, g_router, g_ffn = whole(
        mix_kernel,
        [
            ((1, count, D), BF16),
            ((count, D), F32),
            ((count, D), BF16),
            ((owners * QROW, EXP), F32),
            ((8, D), F32),
        ],
        flops=10**9,
        moved=5 * 10**6,
    )(returned, places, gates, resid, cot, gains, full, normed_ffn, route)

    branch_seq = swap(jnp.broadcast_to(d_branch[None], (2, count, D))).reshape(seq, D)
    chunked = nn(attended, gather_rows).astype(BF16)
    g_output = tn(chunked, branch_seq).astype(BF16)
    g_output = swap(g_output.reshape(owners, SLOT, D), "ep")

    g_pack, d_norm = whole(
        last_kernel,
        [((owners * QROW, PW), BF16), ((seq, D), F32)],
        scratch=[pltpu.VMEM((seq, QW), BF16), pltpu.VMEM((8, seq), F32)],
        flops=5 * 10**9,
        moved=10 * 10**6,
    )(branch_seq, output_mine, qkv_all, lse, bias, normed_attn, sequence, full, turned_buckets, g_router, g_ffn)

    g_pack = swap(g_pack.reshape(owners, QROW, PW), "ep")
    d_parts = swap(d_norm.reshape(2, count, D)).reshape(seq, D)
    (d_tokens,) = whole(end_kernel, [((1, count, D), F32)], flops=10**6, moved=10**6)(d_parts, d_resid, tok, gains)

    grad_w_output = jnp.sum(g_output.astype(F32), axis=0)[:6]
    summed = jnp.sum(g_pack.astype(F32), axis=0)[:12].reshape(2, 6, PW)
    summed = swap(summed)
    weights = summed[:, :, :QW].reshape(2, 6, 3, HW).transpose(2, 1, 0, 3).reshape(3, 6, D)
    both = summed[0, :, QW:] + summed[1, :, QW:]
    extra = both[:, 64:70]
    return (
        mixed,
        d_tokens,
        weights[0],
        weights[1],
        weights[2],
        grad_w_output,
        extra[:, 0] + extra[:, 1],
        extra[:, 2] + extra[:, 3],
        both[:, :EXP],
        (extra[:, 4] + extra[:, 5])[:3],
        grad_w_in,
        grad_w_out,
    )


def solution(mesh):
    wide = P(("sp", "ep"), None)
    flat = P(("sp", "ep"))
    rows = P("ep", "sp", None)
    return jax.shard_map(
        shards,
        mesh=mesh,
        in_specs=(rows, rows, wide, wide, wide, wide, flat, flat, wide, flat, P("ep", None, "sp"), rows, rows, P()),
        out_specs=(rows, rows, wide, wide, wide, wide, flat, flat, wide, flat, P("ep", None, "sp"), rows),
        check_vma=False,
    )
```

time: 1990 us -> 301 us (0.15); the launches traced: 1960 us -> 299 us
  blocking collectives: 894 us -> 126 us
  local copies, waits for them, and re-layouts: 405 us -> 15 us
  starting transfers between devices: 356 us -> 25.9 us
  waiting for transfers between devices: 193 us -> 60.3 us
  matrix products: 70.9 us -> 3.38 us
  Pallas kernels: 0 us -> 64 us
    unnamed x3 -> x0, blocking collectives: 538 us -> none
    all_gather x1 -> x0, blocking collectives: 339 us -> none  [shards(): lax.all_gather(router, ('sp', 'ep'), axis=0, tiled=True)]
    unnamed x129 -> x0, starting transfers between devices: 310 us -> none
    gather x4 -> x0, local copies, waits for them, and re-layouts: 238 us -> none  [the longest x2 235 us: shards(): bias = jnp.take(distance_bias, relative, axis=1)]
    unnamed x134 -> x0, waiting for transfers between devices: 164 us -> none
    all_to_all x4 -> x10, blocking collectives: 17.3 us -> 126 us  [swap(): return lax.all_to_all(values, axis, split_axis=0, concat_axis=0, tiled=True)]
    unnamed x388 -> x20, local copies, waits for them, and re-layouts: 102 us -> 4.25 us
    dot_general x31 -> x3, matrix products: 70.9 us -> 3.38 us  [the longest x2 2.58 us: nn(): lax.dot_general(left, right, (((1,), (0,)), ((), ())), preferred_element_...]
  transfers between devices with their start and end apart: 141 -> 4, of which waited for: 22 -> 4; matrix products, arithmetic and copies ran while one was open for 23% -> 2% of each run, Pallas kernels for 0% -> 5%
where the time goes in v1:
time: 301 us; the launch traced here: 299 us
  blocking collectives  126 us (42%)
  Pallas kernels  64 us (21%)
  waiting for transfers between devices  60.3 us (20%)
  starting transfers between devices  25.9 us (9%)
  local copies, waits for them, and re-layouts  15 us (5%)
  other arithmetic  4.32 us (1%)
  matrix products  3.38 us (1%)
    all_to_all x10, blocking collectives, swap(): return lax.all_to_all(values, axis, split_axis=0, concat_axis=0, tiled=True)  126 us
    all_to_all x4, waiting for transfers between devices, swap(): return lax.all_to_all(values, axis, split_axis=0, concat_axis=0, tiled=True)  60.3 us
    all_to_all x4, starting transfers between devices, swap(): return lax.all_to_all(values, axis, split_axis=0, concat_axis=0, tiled=True)  25.9 us
    pallas_call x1, Pallas kernels, shards(): pl.pallas_call(expert_kernel, grid=(hidden // step,), in_specs=[resident,...  20.9 us
    pallas_call x1, Pallas kernels, shards(): whole(last_kernel, [((owners * QROW, PW), BF16), ((seq, D), F32)], scratc...  11.9 us
    pallas_call x1, Pallas kernels, shards(): pl.pallas_call(expert_grad_kernel, grid=(hidden // step,), in_specs=[resi...  11.7 us
    pallas_call x1, Pallas kernels, shards(): whole(first_kernel, [((seq, HW), BF16), ((seq, QW), BF16), ((D, PW), BF16...  7.37 us
  transfers between devices with their start and end apart: 4, of which 4 were waited for; matrix products, arithmetic and copies ran while one was open for 2% of the time, Pallas kernels for 5%

profile of v1, /device:TPU:1, one launch (start us, length us, event | category | flops | bytes accessed | tf_op | source)
XLA Modules:
  0.0 299.2 jit_solution(5826293517638569)
XLA Ops:
  5.3 4.7 %all-to-all-start.1 = ((bf16[2,6,1280]{2,1,0:T(8,128)(2,1)}), bf16[2,6,1280]{2,1,0:T(8,128)(2,1)S(1)}, u32[]{:S(2)}, u32[]{:S(2)}) async-start(bf16[2,6,1280]{2,1,0:T(8,128)(2,1)} %copy.51), calls=%async_computation.1 | async-start | bytes 81920 | tf_op jit(solution)/shard_map/all_to_all | solution.py:305
  11.9 4.8 %all_to_all.70 = bf16[2,128,768]{2,1,0:T(8,128)(2,1)} all-to-all(bf16[2,128,768]{2,1,0:T(8,128)(2,1)S(1)} %broadcast_in_dim.27), channel_id=1, replica_groups=mesh['sp'=2,'ep'=64] {'sp'}, dimensions={0} | all-to-all | bytes 786432 | tf_op jit(solution)/shard_map/all_to_all | solution.py:305
  17.6 11.2 %all-to-all-start.3 = ((bf16[64,8,768]{2,1,0:T(8,128)(2,1)}), bf16[64,8,768]{2,1,0:T(8,128)(2,1)S(1)}, u32[]{:S(2)}, u32[]{:S(2)}) async-start(bf16[64,8,768]{2,1,0:T(8,128)(2,1)} %broadcast_in_dim.62), calls=%async_computation.3 | async-start | bytes 1572864 | tf_op jit(solution)/shard_map/all_to_all | solution.py:305
  28.9 14.5 %all-to-all-done.3 = bf16[64,8,768]{2,1,0:T(8,128)(2,1)S(1)} async-done(((bf16[64,8,768]{2,1,0:T(8,128)(2,1)}), bf16[64,8,768]{2,1,0:T(8,128)(2,1)S(1)}, u32[]{:S(2)}, u32[]{:S(2)}) %all-to-all-start.3) | async-done | bytes 786464 | tf_op jit(solution)/shard_map/all_to_all | solution.py:305
  45.1 5.0 %all-to-all-start.2 = ((bf16[64,16,1280]{2,1,0:T(8,128)(2,1)}), bf16[64,16,1280]{2,1,0:T(8,128)(2,1)S(1)}, u32[]{:S(2)}, u32[]{:S(2)}) async-start(bf16[64,16,1280]{2,1,0:T(8,128)(2,1)} %broadcast_in_dim.61), calls=%async_computation.2 | async-start | bytes 5242880 | tf_op jit(solution)/shard_map/all_to_all | solution.py:305
  54.2 28.1 %all-to-all-done.2 = bf16[64,16,1280]{2,1,0:T(8,128)(2,1)S(1)} async-done(((bf16[64,16,1280]{2,1,0:T(8,128)(2,1)}), bf16[64,16,1280]{2,1,0:T(8,128)(2,1)S(1)}, u32[]{:S(2)}, u32[]{:S(2)}) %all-to-all-start.2) | async-done | bytes 2621472 | tf_op jit(solution)/shard_map/all_to_all | solution.py:305
  83.8 7.4 %shard_map.229 = (bf16[256,384]{1,0:T(8,128)(2,1)}, bf16[256,1152]{1,0:T(8,128)(2,1)}, bf16[768,1280]{1,0:T(8,128)(2,1)}, f32[128,768]{1,0:T(8,128)}, bf16[256,7...) custom-call(bf16[256,768]{1,0:T(8,128)(2,1)} %bitcast.72, bf16[1024,1280]{1,0:T(8,128)(2,1)} %bitcast.62, ...), custom_call_target="tpu_custom_call" | custom-call | flops 4000000000 | bytes 8000000 | tf_op jit(solution)/shard_map/pallas_call | solution.py:335
  92.5 9.4 %all_to_all.71 = f32[2,128,768]{2,1,0:T(8,128)} all-to-all(f32[2,128,768]{2,1,0:T(8,128)S(1)} %bitcast.61), channel_id=1, replica_groups=mesh['sp'=2,'ep'=64] {'sp'}, dimensions={0} | all-to-all | bytes 1572864 | tf_op jit(solution)/shard_map/all_to_all | solution.py:305
  101.8 4.6 %shard_map.230 = (bf16[512,1536]{1,0:T(8,128)(2,1)}, f32[128,768]{1,0:T(8,128)}, bf16[128,768]{1,0:T(8,128)(2,1)}, bf16[128,1024]{1,0:T(8,128)(2,1)}, f32[128,128]{1,0:T(8,128)}) custom-call(f32[256,768]{1,0:T(8,128)} %bitcast.68, bf16[128,768]{1,0:T(8,128)(2,1)} %bitcast.70, bf16[128,768]{1,0:T(8,128)(2,1)} %bitcast.79, ...), custom_call_target="tpu_custom_call" | custom-call | flops 1000000000 | bytes 4000000 | tf_op jit(solution)/shard_map/pallas_call | solution.py:357
  106.4 27.6 %all_to_all.72 = bf16[64,8,1536]{2,1,0:T(8,128)(2,1)S(1)} all-to-all(bf16[64,8,1536]{2,1,0:T(8,128)(2,1)} %bitcast.64), channel_id=1, replica_groups=mesh['sp'=2,'ep'=64] {'ep'}, dimensions={0} | all-to-all | bytes 3145728 | tf_op jit(solution)/shard_map/all_to_all | solution.py:305
  134.2 9.6 %all_to_all.73 = bf16[2,512,1536]{2,1,0:T(8,128)(2,1)} all-to-all(bf16[2,512,1536]{2,1,0:T(8,128)(2,1)S(1)} %broadcast_in_dim.64), channel_id=1, replica_groups=mesh['sp'=2,'ep'=64] {'sp'}, dimensions={0} | all-to-all | bytes 6291456 | tf_op jit(solution)/shard_map/all_to_all | solution.py:305
  143.9 20.9 %shard_map.231 = (bf16[1024,1536]{1,0:T(8,128)(2,1)}, bf16[1024,1536]{1,0:T(8,128)(2,1)}, bf16[1024,1536]{1,0:T(8,128)(2,1)}) custom-call(bf16[1024,1536]{1,0:T(8,128)(2,1)} %bitcast.57, bf16[768,1536]{1,0:T(8,128)(2,1)} %bitcast.94, bf16[1536,768]{1,0:T(8,128)(2,1)} %bitcast.95), custom_call_target="tpu_custom_call" | custom-call | flops 9663676416 | bytes 20000000 | tf_op jit(solution)/shard_map/pallas_call | solution.py:378
  164.8 7.5 %all_to_all.74 = bf16[2,512,1536]{2,1,0:T(8,128)(2,1)S(1)} all-to-all(bf16[2,512,1536]{2,1,0:T(8,128)(2,1)} %bitcast.59), channel_id=1, replica_groups=mesh['sp'=2,'ep'=64] {'sp'}, dimensions={0} | all-to-all | bytes 6291456 | tf_op jit(solution)/shard_map/all_to_all | solution.py:305
  172.7 27.0 %all_to_all.75 = bf16[64,8,1536]{2,1,0:T(8,128)(2,1)} all-to-all(bf16[64,8,1536]{2,1,0:T(8,128)(2,1)S(1)} %fusion), channel_id=1, replica_groups=mesh['sp'=2,'ep'=64] {'ep'}, dimensions={0} | all-to-all | bytes 3145728 | tf_op jit(solution)/shard_map/all_to_all | solution.py:305
  199.7 5.1 %shard_map.232 = (bf16[1,128,768]{2,1,0:T(8,128)(2,1)}, f32[128,768]{1,0:T(8,128)}, bf16[128,768]{1,0:T(8,128)(2,1)}, f32[1024,64]{1,0:T(8,128)}, f32[8,768]{1,0:T(8,128)}) custom-call(bf16[512,1536]{1,0:T(8,128)(2,1)} %bitcast.55, bf16[128,1024]{1,0:T(8,128)(2,1)} %get-tuple-element.41.places_ref, f32[128,128]{1,0:T(8,128)} %get-tuple-element.42.gates_ref, ...), custom_call_target="tpu_custom_call" | custom-call | flops 1000000000 | bytes 5000000 | tf_op jit(solution)/shard_map/pallas_call | solution.py:417
  205.7 6.4 %all_to_all.76 = bf16[2,128,768]{2,1,0:T(8,128)(2,1)S(1)} all-to-all(bf16[2,128,768]{2,1,0:T(8,128)(2,1)S(1)} %broadcast_in_dim.65), channel_id=1, replica_groups=mesh['sp'=2,'ep'=64] {'sp'}, dimensions={0} | all-to-all | bytes 786432 | tf_op jit(solution)/shard_map/all_to_all | solution.py:305
  212.9 11.9 %shard_map.233 = (bf16[1024,1280]{1,0:T(8,128)(2,1)}, f32[256,768]{1,0:T(8,128)}) custom-call(bf16[256,768]{1,0:T(8,128)(2,1)} %bitcast.66, bf16[384,768]{1,0:T(8,128)(2,1)} %convolution_convert_fusion.1.wo_ref, bf16[256,1152]{1,0:T(8,128)(2,1)} %get-tuple-element.47.qkv_ref, f32[256,128]{1,0:T(8,128)} %get-tuple-element.48.lse_ref, ...), custom_call_target="tpu_custom_call" | custom-call | flops 5000000000 | bytes 10000000 | tf_op jit(solution)/shard_map/pallas_call | solution.py:435
  224.9 6.3 %all_to_all.77 = f32[2,128,768]{2,1,0:T(8,128)} all-to-all(f32[2,128,768]{2,1,0:T(8,128)} %bitcast.67), channel_id=1, replica_groups=mesh['sp'=2,'ep'=64] {'sp'}, dimensions={0} | all-to-all | bytes 1572864 | tf_op jit(solution)/shard_map/all_to_all | solution.py:305
  231.2 19.0 %all_to_all.78 = bf16[64,8,768]{2,1,0:T(8,128)(2,1)S(1)} all-to-all(bf16[64,8,768]{2,1,0:T(8,128)(2,1)S(1)} %fusion.1), channel_id=1, replica_groups=mesh['sp'=2,'ep'=64] {'ep'}, dimensions={0} | all-to-all | bytes 1572864 | tf_op jit(solution)/shard_map/all_to_all | solution.py:305
  250.2 4.9 %all-to-all-start.11 = ((bf16[64,16,1280]{2,1,0:T(8,128)(2,1)}), bf16[64,16,1280]{2,1,0:T(8,128)(2,1)S(1)}, u32[]{:S(2)}, u32[]{:S(2)}) async-start(bf16[64,16,1280]{2,1,0:T(8,128)(2,1)} %bitcast.63), calls=%async_computation.11 | async-start | bytes 5242880 | tf_op jit(solution)/shard_map/all_to_all | solution.py:305
  255.1 11.7 %shard_map.235 = (f32[1,768,1536]{2,1,0:T(8,128)}, f32[1,1536,768]{2,1,0:T(8,128)}) custom-call(bf16[1024,1536]{1,0:T(8,128)(2,1)} %bitcast.58, bf16[1024,1536]{1,0:T(8,128)(2,1)} %get-tuple-element.56.act_ref, bf16[1024,1536]{1,0:T(8,128)(2,1)} %get-tuple-element.57.dpre_ref), custom_call_target="tpu_custom_call" | custom-call | flops 4831838208 | bytes 20000000 | tf_op jit(solution)/shard_map/pallas_call | solution.py:400
  266.9 2.3 shard_map.234
  270.0 17.3 %all-to-all-done.11 = bf16[64,16,1280]{2,1,0:T(8,128)(2,1)S(1)} async-done(((bf16[64,16,1280]{2,1,0:T(8,128)(2,1)}), bf16[64,16,1280]{2,1,0:T(8,128)(2,1)S(1)}, u32[]{:S(2)}, u32[]{:S(2)}) %all-to-all-start.11) | async-done | bytes 2621472 | tf_op jit(solution)/shard_map/all_to_all | solution.py:305
  287.7 8.0 %all_to_all.79 = f32[2,6,1280]{2,1,0:T(8,128)S(1)} all-to-all(f32[2,6,1280]{2,1,0:T(8,128)S(1)} %reshape.146), channel_id=1, replica_groups=mesh['sp'=2,'ep'=64] {'sp'}, dimensions={0} | all-to-all | bytes 122880 | tf_op jit(solution)/shard_map/all_to_all | solution.py:305
  (61 shorter events, 23.0 us)
Async XLA Ops:
  5.3 5.7 %all-to-all-start.1 = ((bf16[2,6,1280]{2,1,0:T(8,128)(2,1)}), bf16[2,6,1280]{2,1,0:T(8,128)(2,1)S(1)}, u32[]{:S(2)}, u32[]{:S(2)}) async-start(bf16[2,6,1280]{2,1,0:T(8,128)(2,1)} %copy.51), calls=%async_computation.1 | async-start | bytes 81920 | tf_op jit(solution)/shard_map/all_to_all | solution.py:305
  17.6 25.8 %all-to-all-start.3 = ((bf16[64,8,768]{2,1,0:T(8,128)(2,1)}), bf16[64,8,768]{2,1,0:T(8,128)(2,1)S(1)}, u32[]{:S(2)}, u32[]{:S(2)}) async-start(bf16[64,8,768]{2,1,0:T(8,128)(2,1)} %broadcast_in_dim.62), calls=%async_computation.3 | async-start | bytes 1572864 | tf_op jit(solution)/shard_map/all_to_all | solution.py:305
  45.1 5.1 %copy-start.6 = (s32[256]{0:T(256)S(1)}, s32[256]{0:T(256)}, u32[]{:S(2)}) copy-start(s32[256]{0:T(256)} %param.27) | copy-start | bytes 3076
  45.1 5.8 %copy-start.5 = (s32[1,128,2]{1,2,0:T(2,128)S(1)}, s32[1,128,2]{1,2,0:T(2,128)}, u32[]{:S(2)}) copy-start(s32[1,128,2]{1,2,0:T(2,128)} %param.26) | copy-start | bytes 3076
  45.1 37.2 %all-to-all-start.2 = ((bf16[64,16,1280]{2,1,0:T(8,128)(2,1)}), bf16[64,16,1280]{2,1,0:T(8,128)(2,1)S(1)}, u32[]{:S(2)}, u32[]{:S(2)}) async-start(bf16[64,16,1280]{2,1,0:T(8,128)(2,1)} %broadcast_in_dim.61), calls=%async_computation.2 | async-start | bytes 5242880 | tf_op jit(solution)/shard_map/all_to_all | solution.py:305
  82.3 1.5 copy-start
  83.8 7.4 %copy-start.3 = (bf16[384,768]{1,0:T(8,128)(2,1)S(1)}, bf16[384,768]{1,0:T(8,128)(2,1)}, u32[]{:S(2)}) copy-start(bf16[384,768]{1,0:T(8,128)(2,1)} %convolution_convert_fusion.1.wo_ref) | copy-start | bytes 1769476
  199.7 12.4 %copy-start.2 = (bf16[256,384]{1,0:T(8,128)(2,1)S(1)}, bf16[256,384]{1,0:T(8,128)(2,1)}, u32[]{:S(2)}) copy-start(bf16[256,384]{1,0:T(8,128)(2,1)} %get-tuple-element.36) | copy-start | bytes 589828
  212.1 0.8 copy-start.1
  250.2 37.1 %all-to-all-start.11 = ((bf16[64,16,1280]{2,1,0:T(8,128)(2,1)}), bf16[64,16,1280]{2,1,0:T(8,128)(2,1)S(1)}, u32[]{:S(2)}, u32[]{:S(2)}) async-start(bf16[64,16,1280]{2,1,0:T(8,128)(2,1)} %bitcast.63), calls=%async_computation.11 | async-start | bytes 5242880 | tf_op jit(solution)/shard_map/all_to_all | solution.py:305
  295.8 3.4 %copy-start.4 = (f32[6,128]{1,0:T(8,128)}, f32[6,128]{1,0:T(8,128)S(1)}, u32[]{:S(2)}) copy-start(f32[6,128]{1,0:T(8,128)S(1)} %fusion.6) | copy-start | bytes 9220

commit v2 on v1

--- a/solution.py
+++ b/solution.py
@@ -18,6 +18,10 @@
 QROW = 16
 QW = 3 * HW
 PW = QW + 128
+SIDE = 4
+STRIDES = (16, 4, 1)
+PARTS = ((0, 512, (2, 1, 0)), (512, 384, (0, 2, 1)), (896, 384, (1, 0, 2)))
+MESH = pl.DeviceIdType.MESH
 ROUTER = QW
 GAIN = QW + 64
 F32 = jnp.float32
@@ -63,13 +67,19 @@
 
 
 def to_chunks():
-    rows = iota((D, EXP * QROW), 1)
-    return hot(chunk_feature(rows) == iota((D, EXP * QROW), 0))
+    return hot(chunk_feature(iota((1, EXP * QROW), 1)) == iota((D, EXP * QROW), 0))
 
 
 def from_chunks():
-    rows = iota((EXP * QROW, D), 0)
-    return hot(chunk_feature(rows) == iota((EXP * QROW, D), 1))
+    return hot(chunk_feature(iota((EXP * QROW, 1), 0)) == iota((EXP * QROW, D), 1))
+
+
+def output_row(channel, half, third):
+    owner = jnp.right_shift(channel * 10923, 16)
+    inner = channel - owner * 6
+    later = (inner >= 3).astype(jnp.int32)
+    row = owner * QROW + 12 + 2 * later + half
+    return jnp.where(inner - 3 * later == third, row, -1)
 
 
 def rms_of(values):
@@ -81,7 +91,7 @@
     return pltpu.roll(row, 0, 1, stride=1, stride_axis=0)
 
 
-def first_kernel(seq_ref, pack_ref, bucket_ref, attended_ref, qkv_ref, full_ref, gains_ref, normed_ref, bias_ref, lse_ref):
+def first_kernel(seq_ref, pack_ref, bucket_ref, branch_ref, output_ref, attended_ref, qkv_ref, full_ref, gains_ref, normed_ref, bias_ref, lse_ref):
     seq = seq_ref.shape[0]
     sp = lax.axis_index("sp")
     spread = to_chunks()
@@ -89,8 +99,7 @@
     tail = pack_ref[:, QW:]
     gains = tn(tail, from_chunks())
     gains_ref[...] = gains
-    rows = iota((EXP * QROW, 128), 0)
-    entry = chunk_entry(rows)
+    entry = chunk_entry(iota((EXP * QROW, 1), 0))
     bucket_of = jnp.right_shift(entry * 5462, 16)
     head_of = entry - bucket_of * H
     column = iota((EXP * QROW, 128), 1)
@@ -99,9 +108,15 @@
         tail[:, 66:67].astype(F32),
         0.0,
     ).astype(BF16)
-    entry_wide = chunk_entry(iota((EXP * QROW, seq), 0))
-    bucket_wide = jnp.where(entry_wide >= 0, jnp.right_shift(entry_wide * 5462, 16), -1)
-    bias_ref[...] = tn(table, hot(bucket_wide == bucket_ref[0:1, :]))[0:8, :]
+    bucket_here = jnp.where(entry >= 0, bucket_of, -1)
+    bias_ref[...] = tn(table, hot(bucket_here == bucket_ref[0:1, :]))[0:8, :]
+    channel = iota((HW, 1), 0)
+    for half in range(2):
+        rows = jnp.zeros((HW, HW), F32)
+        for third in range(3):
+            pick = hot(output_row(channel, half, third) == iota((HW, EXP * QROW), 1))
+            rows = rows + nn(pick, pack_ref[:, third * HW : (third + 1) * HW])
+        output_ref[:, half * HW : (half + 1) * HW] = rows.astype(BF16)
 
     inputs = seq_ref[...].astype(F32)
     normed = (inputs * rms_of(inputs) * gains[64:65, :]).astype(BF16)
@@ -122,6 +137,7 @@
         probs = (grown / total).astype(BF16)
         attended_ref[:, at : at + HD] = nn(probs, value).astype(BF16)
         lse_ref[:, head : head + 1] = peak + jnp.log(total)
+    branch_ref[...] = nn(attended_ref[...], output_ref[...])
 
 
 def route_hot(routes_ref, k, width):
@@ -229,7 +245,7 @@
     return high, (values - high.astype(F32)).astype(BF16)
 
 
-def last_kernel(branch_ref, wo_ref, qkv_ref, lse_ref, bias_ref, normed_ref, seq_ref, full_ref, bucket_ref, grouter_ref, gffn_ref, pack_ref, dnorm_ref, dqkv, ddist):
+def last_kernel(branch_ref, wo_ref, attended_ref, qkv_ref, lse_ref, bias_ref, normed_ref, seq_ref, full_ref, bucket_ref, grouter_ref, gffn_ref, pack_ref, dnorm_ref, dqkv, ddist):
     seq = seq_ref.shape[0]
     sp = lax.axis_index("sp")
     d_attended = nt(branch_ref[...], wo_ref[...]).astype(BF16)
@@ -257,21 +273,27 @@
     dnorm_ref[...] = d_normed
     chunked = nn(normed_ref[...], to_chunks()).astype(BF16)
     turned = chunked.T
-    pack_ref[:, :QW] = nn(turned, dqkv[...]).astype(BF16)
+    g_output = tn(attended_ref[...], branch_ref[...]).astype(BF16)
+    channel = iota((1, HW), 1)
+    for third in range(3):
+        there = slice(third * HW, (third + 1) * HW)
+        total = nn(turned, dqkv[:, there])
+        for half in range(2):
+            place = hot(output_row(channel, half, third) == iota((EXP * QROW, HW), 0))
+            total = total + nn(place, g_output[:, half * HW : (half + 1) * HW])
+        pack_ref[:, there] = total.astype(BF16)
     inputs = seq_ref[...].astype(F32)
     g_first = jnp.sum(d_normed * inputs * rms_of(inputs), axis=0, keepdims=True)
     order = from_chunks()
     first_high, first_low = split_two(jnp.broadcast_to(g_first, (16, D)))
     second_high, second_low = split_two(jnp.broadcast_to(gffn_ref[0:1, :], (16, D)))
     gains = [nt(order, one)[:, 0:1] for one in (first_high, first_low, second_high, second_low)]
-    rows = iota((EXP * QROW, seq), 0)
-    entry = chunk_entry(rows)
-    bucket_wide = jnp.where(entry >= 0, jnp.right_shift(entry * 5462, 16), -1)
-    pick = hot(bucket_wide == bucket_ref[1:2, :])
+    entry = chunk_entry(iota((EXP * QROW, 1), 0))
+    bucket_of = jnp.right_shift(entry * 5462, 16)
+    pick = hot(jnp.where(entry >= 0, bucket_of, -1) == bucket_ref[1:2, :])
     high, low = split_two(ddist[...])
     by_head = nt(pick, high) + nt(pick, low)
-    entry = chunk_entry(iota(by_head.shape, 0))
-    head_of = entry - jnp.right_shift(entry * 5462, 16) * H
+    head_of = entry - bucket_of * H
     mine = (entry >= 0) & (head_of == sp * HH + iota(by_head.shape, 1)) & (iota(by_head.shape, 1) < HH)
     table = jnp.sum(jnp.where(mine, by_head, 0.0), axis=-1, keepdims=True)
     table_high, table_low = split_two(table)
@@ -291,12 +313,178 @@
     out_ref[0] = dresid_ref[...] + rms * v - inputs * (rms * rms * rms) * jnp.mean(v * inputs, axis=-1, keepdims=True)
 
 
-def whole(kernel, outs, scratch=(), flops=0, moved=0):
+def here():
+    owner = lax.axis_index("ep")
+    return (owner // 16, owner // 4 % 4, owner % 4)
+
+
+def across(axis, shift):
+    owner, place = lax.axis_index("ep"), here()[axis]
+    return {"ep": owner + ((place + shift) % SIDE - place) * STRIDES[axis]}
+
+
+def other_core():
+    return {"sp": 1 - lax.axis_index("sp")}
+
+
+def greet():
+    barrier = pltpu.get_barrier_semaphore()
+    pl.semaphore_signal(barrier, inc=1, device_id=other_core(), device_id_type=MESH)
+    for axis in range(3):
+        for shift in range(1, SIDE):
+            pl.semaphore_signal(barrier, inc=1, device_id=across(axis, shift), device_id_type=MESH)
+
+
+def meet():
+    pl.semaphore_wait(pltpu.get_barrier_semaphore(), 1 + 3 * (SIDE - 1))
+
+
+def remote(source, target, send, receive, device):
+    copy = pltpu.make_async_remote_copy(
+        src_ref=source, dst_ref=target, send_sem=send, recv_sem=receive, device_id=device, device_id_type=MESH
+    )
+    copy.start()
+    return copy
+
+
+def gather_kernel(wq_ref, wk_ref, wv_ref, wo_ref, router_ref, attn_ref, ffn_ref, table_ref, tok_ref, pack_ref, seq_ref, stage, got, out16, core_send, core_recv, send, recv):
+    greet()
+    sp = lax.axis_index("sp")
+    place = here()
+    stage[...] = jnp.zeros_like(stage)
+    out16[...] = jnp.zeros_like(out16)
+    out16[0:6, :] = wo_ref[...]
+
+    def standing(ref):
+        size = ref.shape[1]
+        values = jnp.broadcast_to(ref[...].astype(F32), (QROW, size))
+        kept = jnp.where(iota((QROW, size), 0) == iota((QROW, size), 1), values, 0.0)
+        return jnp.sum(kept, axis=1, keepdims=True)
+
+    column = iota((QROW, 64), 1)
+    tail = jnp.where(column == 0, standing(attn_ref), 0.0)
+    tail = jnp.where(column == 1, standing(ffn_ref), tail)
+    tail = jnp.where(column == 2, standing(table_ref), tail).astype(BF16)
+    for half in range(2):
+        for n, ref in enumerate((wq_ref, wk_ref, wv_ref)):
+            stage[half, 0:6, n * HW : (n + 1) * HW] = ref[:, half * HW : (half + 1) * HW]
+        stage[half, 0:6, ROUTER : ROUTER + EXP] = router_ref[...]
+        stage[half, :, GAIN:] = tail
+    seq_ref[sp] = tok_ref[...]
+    meet()
+    chunk_copy = remote(stage.at[1 - sp], got, core_send.at[0], core_recv.at[0], other_core())
+    tok_copy = remote(tok_ref, seq_ref.at[sp], core_send.at[1], core_recv.at[1], other_core())
+    row, col = iota((QROW, QROW), 0), iota((QROW, QROW), 1)
+    low = jnp.where((row == col) & (col < 6), 1.0, 0.0)
+    high = jnp.where((row == col + 6) & (col < 6), 1.0, 0.0)
+    own = jnp.where(sp == 0, low, high).astype(BF16)
+    others = jnp.where(sp == 0, high, low).astype(BF16)
+    later = (col >= 3).astype(jnp.int32)
+    chunk_copy.wait()
+    mine = nn(own, stage[sp]) + nn(others, got[...])
+    pack_ref[place[0], place[1], place[2], :, QW:] = mine[:, QW:].astype(BF16)
+    for third in range(3):
+        there = slice(third * HW, (third + 1) * HW)
+        total = mine[:, there]
+        for half in range(2):
+            pick = hot((col < 6) & (col - 3 * later == third) & (row == 12 + 2 * later + half))
+            total = total + nn(pick, out16[:, half * HW : (half + 1) * HW])
+        pack_ref[place[0], place[1], place[2], :, there] = total.astype(BF16)
+    copies = {}
+    for phase in range(3):
+        for part, (first, width, order) in enumerate(PARTS):
+            index = [pl.ds(0, SIDE) if axis in order[:phase] else place[axis] for axis in range(3)]
+            block = pack_ref.at[index[0], index[1], index[2], :, pl.ds(first, width)]
+            if phase:
+                for shift in range(1, SIDE):
+                    copies[phase - 1, part, shift].wait_recv()
+            for shift in range(1, SIDE):
+                copies[phase, part, shift] = remote(
+                    block, block, send.at[phase, part, shift - 1], recv.at[phase, part, shift - 1], across(order[phase], shift)
+                )
+    for part in range(3):
+        for shift in range(1, SIDE):
+            copies[2, part, shift].wait_recv()
+    for copy in copies.values():
+        copy.wait_send()
+    tok_copy.wait()
+
+
+def reduce_kernel(pack_ref, q_ref, k_ref, v_ref, o_ref, rest_ref, *scratch):
+    firsts, sums, seconds, pairs, thirds = (scratch[3 * n : 3 * n + 3] for n in range(5))
+    total, theirs, core_send, core_recv, send, recv = scratch[15:]
+    greet()
+    sp = lax.axis_index("sp")
+    place = here()
+    meet()
+    copies = {}
+
+    def push(phase, part, axis, shift, source, target):
+        copies[phase, part, shift] = remote(
+            source,
+            target.at[shift - 1],
+            send.at[phase, part, shift - 1],
+            recv.at[phase, part, shift - 1],
+            across(axis, shift),
+        )
+
+    def added(phase, part, own, arrived):
+        values = own.astype(F32)
+        for shift in range(1, SIDE):
+            copies[phase, part, shift].wait_recv()
+            values = values + arrived[shift - 1].astype(F32)
+        return values
+
+    def at(axes, axis, value):
+        return tuple(value if one == axis else pl.ds(0, SIDE) for one in axes)
+
+    for part, (first, width, order) in enumerate(PARTS):
+        axis = order[2]
+        for shift in (2, 1, 3):
+            index = at((0, 1, 2), axis, (place[axis] + shift) % SIDE)
+            push(0, part, axis, shift, pack_ref.at[index + (slice(None), pl.ds(first, width))], firsts[part])
+    for part, (first, width, order) in enumerate(PARTS):
+        own = pack_ref[at((0, 1, 2), order[2], place[order[2]]) + (slice(None), pl.ds(first, width))]
+        sums[part][...] = added(0, part, own, firsts[part]).astype(BF16)
+        axis = order[1]
+        for shift in (2, 1, 3):
+            index = at(sorted(order[:2]), axis, (place[axis] + shift) % SIDE)
+            push(1, part, axis, shift, sums[part].at[index], seconds[part])
+    for part, (first, width, order) in enumerate(PARTS):
+        own = sums[part][at(sorted(order[:2]), order[1], place[order[1]])]
+        pairs[part][...] = added(1, part, own, seconds[part]).astype(BF16)
+        axis = order[0]
+        for shift in (2, 1, 3):
+            push(2, part, axis, shift, pairs[part].at[(place[axis] + shift) % SIDE], thirds[part])
+    for part, (first, width, order) in enumerate(PARTS):
+        own = pairs[part][place[order[0]]]
+        total[:, first : first + width] = added(2, part, own, thirds[part])
+    core = remote(total, theirs, core_send, core_recv, other_core())
+    for row in range(6):
+        for half in range(2):
+            there = 12 + row // 3 * 2 + half
+            third = row % 3 * HW
+            o_ref[row : row + 1, half * HW : (half + 1) * HW] = total[there : there + 1, third : third + HW]
+    core.wait_recv()
+    mine = jnp.where(sp == 0, total[0:6, :], total[6:12, :])
+    other = jnp.where(sp == 0, theirs[0:6, :], theirs[6:12, :])
+    for n, ref in enumerate((q_ref, k_ref, v_ref)):
+        there = slice(n * HW, (n + 1) * HW)
+        ref[:, :HW] = jnp.where(sp == 0, mine[:, there], other[:, there])
+        ref[:, HW:] = jnp.where(sp == 0, other[:, there], mine[:, there])
+    rest_ref[...] = mine[:, QW:] + other[:, QW:]
+    core.wait_send()
+    for copy in copies.values():
+        copy.wait_send()
+
+
+def whole(kernel, outs, scratch=(), flops=0, moved=0, collective=None):
+    remote_params = {} if collective is None else {"collective_id": collective, "has_side_effects": True}
     return pl.pallas_call(
         kernel,
         out_shape=[jax.ShapeDtypeStruct(shape, kind) for shape, kind in outs],
         scratch_shapes=list(scratch),
-        compiler_params=pltpu.CompilerParams(vmem_limit_bytes=VMEM_LIMIT),
+        compiler_params=pltpu.CompilerParams(vmem_limit_bytes=VMEM_LIMIT, **remote_params),
         cost_estimate=pl.CostEstimate(flops=flops, bytes_accessed=moved, transcendentals=0),
     )
 
@@ -312,29 +500,31 @@
     tok = tokens[0]
     cot = cotangent[0]
     route = routes[0]
-    qkv = jnp.concatenate([w_query, w_key, w_value], axis=1).reshape(6, 3, 2, HW)
-    qkv = qkv.transpose(2, 0, 1, 3).reshape(2, 6, QW)
-    tail = jnp.concatenate(
-        [
-            router,
-            gain_attn[:, None],
-            gain_ffn[:, None],
-            jnp.pad(bias_table, (0, 3))[:, None],
-            jnp.zeros((6, 61), BF16),
-        ],
-        axis=1,
-    )
-    chunk = jnp.concatenate([qkv, jnp.broadcast_to(tail[None], (2, 6, 128))], axis=2)
-    chunk = jnp.pad(swap(chunk).reshape(12, PW), ((0, QROW - 12), (0, 0)))
-    pack = swap(jnp.broadcast_to(chunk[None], (owners, QROW, PW)), "ep").reshape(owners * QROW, PW)
-    out_chunk = jnp.pad(w_output, ((0, SLOT - 6), (0, 0)))
-    out_pack = swap(jnp.broadcast_to(out_chunk[None], (owners, SLOT, D)), "ep").reshape(owners * SLOT, D)
-    sequence = swap(jnp.broadcast_to(tok[None], (2, count, D))).reshape(seq, D)
+    pack, sequence = whole(
+        gather_kernel,
+        [((SIDE, SIDE, SIDE, QROW, PW), BF16), ((2, count, D), BF16)],
+        scratch=[
+            pltpu.VMEM((2, QROW, PW), BF16),
+            pltpu.VMEM((QROW, PW), BF16),
+            pltpu.VMEM((QROW, D), BF16),
+            pltpu.SemaphoreType.DMA((2,)),
+            pltpu.SemaphoreType.DMA((2,)),
+            pltpu.SemaphoreType.DMA((3, 3, SIDE - 1)),
+            pltpu.SemaphoreType.DMA((3, 3, SIDE - 1)),
+        ],
+        flops=10**6,
+        moved=6 * 10**6,
+        collective=0,
+    )(w_query, w_key, w_value, w_output, router, gain_attn[None], gain_ffn[None], bias_table[None], tok)
+    pack = pack.reshape(owners * QROW, PW)
+    sequence = sequence.reshape(seq, D)
     turned_buckets = jnp.stack([jnp.roll(buckets[::-1], 1), jnp.roll(buckets, -1)])
 
-    attended, qkv_all, full, gains, normed_attn, bias, lse = whole(
+    branch, output_mine, attended, qkv_all, full, gains, normed_attn, bias, lse = whole(
         first_kernel,
         [
+            ((seq, D), F32),
+            ((HW, D), BF16),
             ((seq, HW), BF16),
             ((seq, QW), BF16),
             ((D, PW), BF16),
@@ -347,11 +537,6 @@
         moved=8 * 10**6,
     )(sequence, pack, turned_buckets)
 
-    place = jnp.arange(owners * SLOT, dtype=jnp.int32)
-    owner_row = jnp.where(place % SLOT < 6, place // SLOT * 6 + place % SLOT, -1)
-    gather_rows = (owner_row[None, :] == jnp.arange(HW, dtype=jnp.int32)[:, None]).astype(BF16)
-    output_mine = nn(gather_rows, out_pack).astype(BF16)
-    branch = nn(attended, output_mine)
     parts = swap(branch.reshape(2, count, D)).reshape(seq, D)
 
     filled, resid, normed_ffn, places, gates = whole(
@@ -428,38 +613,44 @@
     )(returned, places, gates, resid, cot, gains, full, normed_ffn, route)
 
     branch_seq = swap(jnp.broadcast_to(d_branch[None], (2, count, D))).reshape(seq, D)
-    chunked = nn(attended, gather_rows).astype(BF16)
-    g_output = tn(chunked, branch_seq).astype(BF16)
-    g_output = swap(g_output.reshape(owners, SLOT, D), "ep")
-
     g_pack, d_norm = whole(
         last_kernel,
         [((owners * QROW, PW), BF16), ((seq, D), F32)],
         scratch=[pltpu.VMEM((seq, QW), BF16), pltpu.VMEM((8, seq), F32)],
         flops=5 * 10**9,
         moved=10 * 10**6,
-    )(branch_seq, output_mine, qkv_all, lse, bias, normed_attn, sequence, full, turned_buckets, g_router, g_ffn)
-
-    g_pack = swap(g_pack.reshape(owners, QROW, PW), "ep")
+    )(branch_seq, output_mine, attended, qkv_all, lse, bias, normed_attn, sequence, full, turned_buckets, g_router, g_ffn)
+
     d_parts = swap(d_norm.reshape(2, count, D)).reshape(seq, D)
     (d_tokens,) = whole(end_kernel, [((1, count, D), F32)], flops=10**6, moved=10**6)(d_parts, d_resid, tok, gains)
 
-    grad_w_output = jnp.sum(g_output.astype(F32), axis=0)[:6]
-    summed = jnp.sum(g_pack.astype(F32), axis=0)[:12].reshape(2, 6, PW)
-    summed = swap(summed)
-    weights = summed[:, :, :QW].reshape(2, 6, 3, HW).transpose(2, 1, 0, 3).reshape(3, 6, D)
-    both = summed[0, :, QW:] + summed[1, :, QW:]
-    extra = both[:, 64:70]
+    widths = [width for _, width, _ in PARTS]
+    g_query, g_key, g_value, g_output, rest = whole(
+        reduce_kernel,
+        [((6, D), F32)] * 4 + [((6, 128), F32)],
+        scratch=[pltpu.VMEM((SIDE - 1, SIDE, SIDE, QROW, width), BF16) for width in widths]
+        + [pltpu.VMEM((SIDE, SIDE, QROW, width), BF16) for width in widths]
+        + [pltpu.VMEM((SIDE - 1, SIDE, QROW, width), BF16) for width in widths]
+        + [pltpu.VMEM((SIDE, QROW, width), BF16) for width in widths]
+        + [pltpu.VMEM((SIDE - 1, QROW, width), BF16) for width in widths]
+        + [pltpu.VMEM((QROW, PW), F32)] * 2
+        + [pltpu.SemaphoreType.DMA] * 2
+        + [pltpu.SemaphoreType.DMA((3, 3, SIDE - 1))] * 2,
+        flops=10**7,
+        moved=6 * 10**6,
+        collective=1,
+    )(g_pack.reshape(SIDE, SIDE, SIDE, QROW, PW))
+    extra = rest[:, 64:70]
     return (
         mixed,
         d_tokens,
-        weights[0],
-        weights[1],
-        weights[2],
-        grad_w_output,
+        g_query,
+        g_key,
+        g_value,
+        g_output,
         extra[:, 0] + extra[:, 1],
         extra[:, 2] + extra[:, 3],
-        both[:, :EXP],
+        rest[:, :EXP],
         (extra[:, 4] + extra[:, 5])[:3],
         grad_w_in,
         grad_w_out,

time: 301 us -> 227 us (0.75)
  blocking collectives: 126 us -> 53.2 us
  Pallas kernels: 64 us -> 130 us
  waiting for transfers between devices: 60.3 us -> 13 us
  starting transfers between devices: 25.9 us -> 14.2 us
  local copies, waits for them, and re-layouts: 15 us -> 10.7 us
  matrix products: 3.38 us -> 0 us
    all_to_all x10 -> x4, blocking collectives: 126 us -> 53.2 us  [swap(): return lax.all_to_all(values, axis, split_axis=0, concat_axis=0, tiled=True)]
    pallas_call x1 -> x3, Pallas kernels: 7.37 us -> 69.5 us  [the longest x1 31.6 us: shards(): whole(gather_kernel, [((SIDE, SIDE, SIDE, QROW, PW), BF16), ((2, count, D...]
    all_to_all x4 -> x3, waiting for transfers between devices: 60.3 us -> 13 us  [swap(): return lax.all_to_all(values, axis, split_axis=0, concat_axis=0, tiled=True)]
    all_to_all x4 -> x3, starting transfers between devices: 25.9 us -> 14.2 us  [swap(): return lax.all_to_all(values, axis, split_axis=0, concat_axis=0, tiled=True)]
    broadcast_in_dim x9 -> x0, local copies, waits for them, and re-layouts: 5.83 us -> none  [the longest x1 1.66 us: shards(): jnp.broadcast_to(chunk[None], (owners, QROW, PW))]
    pallas_call x1, Pallas kernels: 11.9 us -> 15.4 us  [shards(): whole(last_kernel, [((owners * QROW, PW), BF16), ((seq, D), F32)], scratc...]
    dot_general x3 -> x0, matrix products: 3.38 us -> none  [the longest x2 2.58 us: nn(): lax.dot_general(left, right, (((1,), (0,)), ((), ())), preferred_element_...]
    unnamed x20 -> x26, local copies, waits for them, and re-layouts: 4.25 us -> 6.94 us
  transfers between devices with their start and end apart: 4 -> 3, of which waited for: 4 -> 3; matrix products, arithmetic and copies ran while one was open for 2% -> 0% of each run, Pallas kernels for 5% -> 5%
where the time goes in v2:
time: 227 us; the launch traced here: 226 us
  Pallas kernels  130 us (57%)
  blocking collectives  53.2 us (23%)
  starting transfers between devices  14.2 us (6%)
  waiting for transfers between devices  13 us (6%)
  local copies, waits for them, and re-layouts  10.7 us (5%)
  other arithmetic  4.55 us (2%)
    all_to_all x4, blocking collectives, swap(): return lax.all_to_all(values, axis, split_axis=0, concat_axis=0, tiled=True)  53.2 us
    pallas_call x1, Pallas kernels, shards(): whole(gather_kernel, [((SIDE, SIDE, SIDE, QROW, PW), BF16), ((2, count, D...  31.6 us
    pallas_call x1, Pallas kernels, shards(): whole(reduce_kernel, [((6, D), F32)] * 4 + [((6, 128), F32)], scratch=[pl...  27.9 us
    pallas_call x1, Pallas kernels, shards(): pl.pallas_call(expert_kernel, grid=(hidden // step,), in_specs=[resident,...  20.9 us
    pallas_call x1, Pallas kernels, shards(): whole(last_kernel, [((owners * QROW, PW), BF16), ((seq, D), F32)], scratc...  15.4 us
    all_to_all x3, starting transfers between devices, swap(): return lax.all_to_all(values, axis, split_axis=0, concat_axis=0, tiled=True)  14.2 us
    all_to_all x3, waiting for transfers between devices, swap(): return lax.all_to_all(values, axis, split_axis=0, concat_axis=0, tiled=True)  13 us
    pallas_call x1, Pallas kernels, shards(): pl.pallas_call(expert_grad_kernel, grid=(hidden // step,), in_specs=[resi...  11.7 us
  transfers between devices with their start and end apart: 3, of which 3 were waited for; matrix products, arithmetic and copies ran while one was open for 0% of the time, Pallas kernels for 5%

profile of v2, /device:TPU:1, one launch (start us, length us, event | category | flops | bytes accessed | tf_op | source)
XLA Modules:
  0.0 225.9 jit_solution(18320296733845964181)
XLA Ops:
  0.6 1.2 slice.56
  4.1 31.6 %shard_map.229 = (bf16[4,4,4,16,1280]{4,3,2,1,0:T(8,128)(2,1)}, bf16[2,128,768]{2,1,0:T(8,128)(2,1)}) custom-call(bf16[6,768]{1,0:T(8,128)(2,1)} %wq_ref.1, bf16[6,768]{1,0:T(8,128)(2,1)} %wk_ref.1, bf16[6,768]{1,0:T(8,128)(2,1)} %wv_ref.1, bf16[6,768]{1,0:T(8,128)(2,1)} %wo_ref.1, bf16[6,64]{1,0:T(8,128)(2,1)} %router_ref.1, bf16[1,6]{1,0:T(2,128)(2,1)} %bitcast.50, ...), custom_call_target="tpu_custom_call" | custom-call | flops 1000000 | bytes 6000000 | tf_op jit(solution)/shard_map/pallas_call | solution.py:503
  35.7 10.0 %shard_map.230 = (f32[256,768]{1,0:T(8,128)}, bf16[384,768]{1,0:T(8,128)(2,1)}, bf16[256,384]{1,0:T(8,128)(2,1)}, bf16[256,1152]{1,0:T(8,128)(2,1)}, bf16[768,12...) custom-call(bf16[256,768]{1,0:T(8,128)(2,1)} %bitcast.56, ...), custom_call_target="tpu_custom_call" | custom-call | flops 4000000000 | bytes 8000000 | tf_op jit(solution)/shard_map/pallas_call | solution.py:523
  45.7 5.8 %all-to-all-start = ((f32[2,128,768]{2,1,0:T(8,128)}), f32[2,128,768]{2,1,0:T(8,128)S(1)}, u32[]{:S(2)}, u32[]{:S(2)}) async-start(f32[2,128,768]{2,1,0:T(8,128)} %bitcast.36), calls=%async_computation | async-start | bytes 1572864 | tf_op jit(solution)/shard_map/all_to_all | solution.py:493
  54.0 4.6 %shard_map.231 = (bf16[512,1536]{1,0:T(8,128)(2,1)}, f32[128,768]{1,0:T(8,128)}, bf16[128,768]{1,0:T(8,128)(2,1)}, bf16[128,1024]{1,0:T(8,128)(2,1)}, f32[128,128]{1,0:T(8,128)}) custom-call(f32[256,768]{1,0:T(8,128)} %bitcast.37, bf16[128,768]{1,0:T(8,128)(2,1)} %bitcast.39, bf16[128,768]{1,0:T(8,128)(2,1)} %bitcast.45, ...), custom_call_target="tpu_custom_call" | custom-call | flops 1000000000 | bytes 4000000 | tf_op jit(solution)/shard_map/pallas_call | solution.py:542
  58.6 28.8 %all_to_all.35 = bf16[64,8,1536]{2,1,0:T(8,128)(2,1)S(1)} all-to-all(bf16[64,8,1536]{2,1,0:T(8,128)(2,1)} %bitcast.34), channel_id=1, replica_groups=mesh['sp'=2,'ep'=64] {'ep'}, dimensions={0} | all-to-all | bytes 3145728 | tf_op jit(solution)/shard_map/all_to_all | solution.py:493
  87.6 9.7 %all_to_all.36 = bf16[2,512,1536]{2,1,0:T(8,128)(2,1)} all-to-all(bf16[2,512,1536]{2,1,0:T(8,128)(2,1)S(1)} %broadcast_in_dim.26), channel_id=1, replica_groups=mesh['sp'=2,'ep'=64] {'sp'}, dimensions={0} | all-to-all | bytes 6291456 | tf_op jit(solution)/shard_map/all_to_all | solution.py:493
  97.2 20.9 %shard_map.232 = (bf16[1024,1536]{1,0:T(8,128)(2,1)}, bf16[1024,1536]{1,0:T(8,128)(2,1)}, bf16[1024,1536]{1,0:T(8,128)(2,1)}) custom-call(bf16[1024,1536]{1,0:T(8,128)(2,1)} %bitcast.29, bf16[768,1536]{1,0:T(8,128)(2,1)} %bitcast.54, bf16[1536,768]{1,0:T(8,128)(2,1)} %bitcast.55), custom_call_target="tpu_custom_call" | custom-call | flops 9663676416 | bytes 20000000 | tf_op jit(solution)/shard_map/pallas_call | solution.py:563
  118.2 7.5 %all_to_all.37 = bf16[2,512,1536]{2,1,0:T(8,128)(2,1)S(1)} all-to-all(bf16[2,512,1536]{2,1,0:T(8,128)(2,1)} %bitcast.31), channel_id=1, replica_groups=mesh['sp'=2,'ep'=64] {'sp'}, dimensions={0} | all-to-all | bytes 6291456 | tf_op jit(solution)/shard_map/all_to_all | solution.py:493
  125.7 1.6 fusion
  127.2 4.7 %all-to-all-start.4 = ((bf16[64,8,1536]{2,1,0:T(8,128)(2,1)}), bf16[64,8,1536]{2,1,0:T(8,128)(2,1)S(1)}, u32[]{:S(2)}, u32[]{:S(2)}) async-start(bf16[64,8,1536]{2,1,0:T(8,128)(2,1)} %fusion), calls=%async_computation.4 | async-start | bytes 3145728 | tf_op jit(solution)/shard_map/all_to_all | solution.py:493
  131.9 11.7 %shard_map.237 = (f32[1,768,1536]{2,1,0:T(8,128)}, f32[1,1536,768]{2,1,0:T(8,128)}) custom-call(bf16[1024,1536]{1,0:T(8,128)(2,1)} %bitcast.30, bf16[1024,1536]{1,0:T(8,128)(2,1)} %get-tuple-element.74.act_ref, bf16[1024,1536]{1,0:T(8,128)(2,1)} %get-tuple-element.75.dpre_ref), custom_call_target="tpu_custom_call" | custom-call | flops 4831838208 | bytes 20000000 | tf_op jit(solution)/shard_map/pallas_call | solution.py:585
  143.7 10.7 %all-to-all-done.4 = bf16[64,8,1536]{2,1,0:T(8,128)(2,1)S(1)} async-done(((bf16[64,8,1536]{2,1,0:T(8,128)(2,1)}), bf16[64,8,1536]{2,1,0:T(8,128)(2,1)S(1)}, u32[]{:S(2)}, u32[]{:S(2)}) %all-to-all-start.4) | async-done | bytes 1572896 | tf_op jit(solution)/shard_map/all_to_all | solution.py:493
  154.3 1.2 copy-done
  155.5 5.1 %shard_map.233 = (bf16[1,128,768]{2,1,0:T(8,128)(2,1)}, f32[128,768]{1,0:T(8,128)}, bf16[128,768]{1,0:T(8,128)(2,1)}, f32[1024,64]{1,0:T(8,128)}, f32[8,768]{1,0:T(8,128)}) custom-call(bf16[512,1536]{1,0:T(8,128)(2,1)} %bitcast.27, bf16[128,1024]{1,0:T(8,128)(2,1)} %get-tuple-element.52.places_ref, f32[128,128]{1,0:T(8,128)} %get-tuple-element.53.gates_ref, ...), custom_call_target="tpu_custom_call" | custom-call | flops 1000000000 | bytes 5000000 | tf_op jit(solution)/shard_map/pallas_call | solution.py:602
  160.6 1.0 broadcast_in_dim.27
  161.5 7.3 %all_to_all.38 = bf16[2,128,768]{2,1,0:T(8,128)(2,1)} all-to-all(bf16[2,128,768]{2,1,0:T(8,128)(2,1)S(1)} %broadcast_in_dim.27), channel_id=1, replica_groups=mesh['sp'=2,'ep'=64] {'sp'}, dimensions={0} | all-to-all | bytes 786432 | tf_op jit(solution)/shard_map/all_to_all | solution.py:493
  168.8 15.4 %shard_map.234 = (bf16[1024,1280]{1,0:T(8,128)(2,1)}, f32[256,768]{1,0:T(8,128)}) custom-call(bf16[256,768]{1,0:T(8,128)(2,1)} %bitcast.41, bf16[384,768]{1,0:T(8,128)(2,1)} %get-tuple-element.58.wo_ref, bf16[256,384]{1,0:T(8,128)(2,1)} %get-tuple-element.59.attended_ref, bf16[256,1152]{1,0:T(8,128)(2,1)} %get-tuple-element.60.qkv_ref, ...), custom_call_target="tpu_custom_call" | custom-call | flops 5000000000 | bytes 10000000 | tf_op jit(solution)/shard_map/pallas_call | solution.py:616
  184.2 27.9 %shard_map.236 = (f32[6,768]{1,0:T(8,128)}, f32[6,768]{1,0:T(8,128)}, f32[6,768]{1,0:T(8,128)}, f32[6,768]{1,0:T(8,128)}, f32[6,128]{1,0:T(8,128)}) custom-call(bf16[4,4,4,16,1280]{4,3,2,1,0:T(8,128)(2,1)} %bitcast.33), custom_call_target="tpu_custom_call" | custom-call | flops 10000000 | bytes 6000000 | tf_op jit(solution)/shard_map/pallas_call | solution.py:628
  212.1 1.6 add_reduce_fusion
  214.4 3.7 %all-to-all-start.6 = ((f32[2,128,768]{2,1,0:T(8,128)}), f32[2,128,768]{2,1,0:T(8,128)S(1)}, u32[]{:S(2)}, u32[]{:S(2)}) async-start(f32[2,128,768]{2,1,0:T(8,128)} %bitcast.35), calls=%async_computation.6 | async-start | bytes 1572864 | tf_op jit(solution)/shard_map/all_to_all | solution.py:493
  218.1 1.6 all-to-all-done.6
  219.6 0.9 copy-done.1
  220.5 2.3 %shard_map.235 = f32[1,128,768]{2,1,0:T(8,128)} custom-call(f32[256,768]{1,0:T(8,128)} %bitcast.32, f32[128,768]{1,0:T(8,128)} %get-tuple-element.67.dresid_ref, bf16[128,768]{1,0:T(8,128)(2,1)} %bitcast.40, f32[128,768]{1,0:T(8,128)} %get-tuple-element.48.gains_ref), custom_call_target="tpu_custom_call" | custom-call | flops 1000000 | bytes 1000000 | tf_op jit(solution)/shard_map/pallas_call | solution.py:625
  (30 shorter events, 8.5 us)
Async XLA Ops:
  35.7 15.9 %copy-start.8 = (s32[1,128,2]{1,2,0:T(2,128)S(1)}, s32[1,128,2]{1,2,0:T(2,128)}, u32[]{:S(2)}) copy-start(s32[1,128,2]{1,2,0:T(2,128)} %param.26) | copy-start | bytes 3076
  45.7 7.4 %all-to-all-start = ((f32[2,128,768]{2,1,0:T(8,128)}), f32[2,128,768]{2,1,0:T(8,128)S(1)}, u32[]{:S(2)}, u32[]{:S(2)}) async-start(f32[2,128,768]{2,1,0:T(8,128)} %bitcast.36), calls=%async_computation | async-start | bytes 1572864 | tf_op jit(solution)/shard_map/all_to_all | solution.py:493
  53.1 0.9 copy-start.2
  127.2 27.1 %all-to-all-start.4 = ((bf16[64,8,1536]{2,1,0:T(8,128)(2,1)}), bf16[64,8,1536]{2,1,0:T(8,128)(2,1)S(1)}, u32[]{:S(2)}, u32[]{:S(2)}) async-start(bf16[64,8,1536]{2,1,0:T(8,128)(2,1)} %fusion), calls=%async_computation.4 | async-start | bytes 3145728 | tf_op jit(solution)/shard_map/all_to_all | solution.py:493
  154.3 1.2 copy-start
  212.1 10.8 %copy-start.7 = (f32[6,768]{1,0:T(8,128)S(1)}, f32[6,768]{1,0:T(8,128)}, u32[]{:S(2)}) copy-start(f32[6,768]{1,0:T(8,128)} %get-tuple-element.97) | copy-start | bytes 55300
  212.1 11.4 %copy-start.6 = (f32[6,768]{1,0:T(8,128)S(1)}, f32[6,768]{1,0:T(8,128)}, u32[]{:S(2)}) copy-start(f32[6,768]{1,0:T(8,128)} %get-tuple-element.98) | copy-start | bytes 55300
  212.1 12.0 %copy-start.5 = (f32[6,768]{1,0:T(8,128)S(1)}, f32[6,768]{1,0:T(8,128)}, u32[]{:S(2)}) copy-start(f32[6,768]{1,0:T(8,128)} %get-tuple-element.99) | copy-start | bytes 55300
  212.1 12.6 %copy-start.4 = (f32[6,768]{1,0:T(8,128)S(1)}, f32[6,768]{1,0:T(8,128)}, u32[]{:S(2)}) copy-start(f32[6,768]{1,0:T(8,128)} %get-tuple-element.100) | copy-start | bytes 55300
  212.1 13.2 %copy-start.3 = (f32[6,128]{1,0:T(8,128)S(1)}, f32[6,128]{1,0:T(8,128)}, u32[]{:S(2)}) copy-start(f32[6,128]{1,0:T(8,128)} %get-tuple-element.73) | copy-start | bytes 9220
  214.4 5.2 %all-to-all-start.6 = ((f32[2,128,768]{2,1,0:T(8,128)}), f32[2,128,768]{2,1,0:T(8,128)S(1)}, u32[]{:S(2)}, u32[]{:S(2)}) async-start(f32[2,128,768]{2,1,0:T(8,128)} %bitcast.35), calls=%async_computation.6 | async-start | bytes 1572864 | tf_op jit(solution)/shard_map/all_to_all | solution.py:493
  219.6 0.9 copy-start.1
